TPU v7x, 128 devices: a whole 4x4x4 slice. The times are simulated.
128 devices in a mesh: energy: 16 (over y, z_lo, core), momentum: 8 (over z_hi, x).
Axes of the slice: x: 4, y: 4, z: 4 (z_hi: 2, z_lo: 2; z = z_hi * 2 + z_lo), core: 2. Of those that a mesh axis runs over, the one named last changes fastest.
Arguments:
- green_blocks: float32 [2, 16, 8, 200, 1024], P(None, 'energy', 'momentum'), may hold values from -6 to 6
- couple_matrix: float32 [3, 100, 1024], P(None, None, ('energy', 'momentum')), may hold values from -1.8 to 1.8
- occupation: float32 [3], replicated, may hold values from 0.1 to 3
- energy_shift: int32 [3], replicated, may hold values from 1 to 15, as said below
- branch_weight: float32 [8, 3], replicated, may hold values from 0.3 to 3
- pair_branch: int32 [8, 8], replicated, may hold values from 0 to 7
Outputs:
- self_energy: float32 [2, 16, 8, 200, 1024], P(None, 'energy', 'momentum')
Inputs may be any that keep to these rules, and one draw needn't show every extreme that they name: `energy_shift`: the branches' shifts are distinct.
All inputs are finite; a program needn't handle non-finite values.
Results may differ from a plain program's by a relative error of at most 0.0001.
Values sent between devices are 32-bit elements; how exact they have to be, the bound alone decides.
No kernel may reach another device: no remote copies, remote signals or barrier semaphores. Data moves between devices by JAX's collectives and lax.ppermute only.
A program may use at most 192 MiB of HBM per device.

v0:
```python
import jax
import jax.numpy as jnp
import numpy as np
from jax import lax
from jax.experimental import pallas as pl
from jax.experimental.pallas import tpu as pltpu
from jax.sharding import PartitionSpec as P

ORB = 10
PAIRS = ORB * ORB
LANES = 128
ATOMS_HERE = 8
ROWS = 25
POINTS = 128
MODES = 3
AXES = ("energy", "momentum")
HIGHEST = lax.Precision.HIGHEST
PARAMS = pltpu.CompilerParams(vmem_limit_bytes=48 * 1024 * 1024)


def split(value):
    high = value.astype(jnp.bfloat16)
    low = (value - high.astype(jnp.float32)).astype(jnp.bfloat16)
    return high, low


def dot(left, right):
    return lax.dot(left, right, preferred_element_type=jnp.float32)


def pack_kernel(green_ref, out_ref, rest_ref):
    for tile in range(3):
        turned = green_ref[LANES * tile : LANES * (tile + 1), :].T
        for owner in range(16):
            out_ref[ROWS * owner + 8 * tile : ROWS * owner + 8 * tile + 8, :] = turned[
                8 * owner : 8 * owner + 8, :
            ]
    rest = green_ref[384:400, :]
    rest_ref[...] = jnp.concatenate([rest, jnp.zeros((112, LANES), jnp.float32)], axis=0).T
    total = rest_ref[pl.ds(0, 16, stride=8), :]
    for atom in range(1, 8):
        total = total + pltpu.roll(rest_ref[pl.ds(atom, 16, stride=8), :], 16 * atom, 1)
    out_ref[pl.ds(24, 16, stride=ROWS), :] = total


def unpack_kernel(in_ref, out_ref, rest_ref):
    for tile in range(3):
        pieces = [
            in_ref[ROWS * owner + 8 * tile : ROWS * owner + 8 * tile + 8, :]
            for owner in range(16)
        ]
        out_ref[LANES * tile : LANES * (tile + 1), :] = jnp.concatenate(pieces, axis=0).T
    rest = in_ref[pl.ds(24, 16, stride=ROWS), :]
    rest_ref[pl.ds(0, 16, stride=8), :] = rest
    for atom in range(1, 8):
        rest_ref[pl.ds(atom, 16, stride=8), :] = pltpu.roll(rest, LANES - 16 * atom, 1)
    out_ref[384:400, :] = rest_ref[...].T[:16, :]


def prepare_kernel(
    occ_ref, shift_ref, couple_ref, mix_ref, cols_ref, rows_ref, out_ref, high_ref, low_ref
):
    spread = lax.dot(
        couple_ref[...], cols_ref[...], precision=HIGHEST, preferred_element_type=jnp.float32
    )
    for index in range(ATOMS_HERE * MODES):
        atom, mode = index // MODES, index % MODES
        part = spread[16 * index : 16 * index + 16, :]
        first = lax.dot(
            rows_ref[:LANES, :], part[:, :LANES], precision=HIGHEST,
            preferred_element_type=jnp.float32,
        )
        second = lax.dot(
            rows_ref[LANES:, :], part[:, LANES:], precision=HIGHEST,
            preferred_element_type=jnp.float32,
        )
        high, low = split(first * second)
        base = 2 * LANES * mode
        out_ref[atom, base : base + LANES, :LANES] = high
        out_ref[atom, base : base + LANES, LANES:] = low
        out_ref[atom, base + LANES : base + 2 * LANES, :LANES] = high
        out_ref[atom, base + LANES : base + 2 * LANES, LANES:] = jnp.zeros_like(low)
    row = lax.broadcasted_iota(jnp.int32, (POINTS, POINTS), 0) >> 3
    col = lax.broadcasted_iota(jnp.int32, (POINTS, POINTS), 1) >> 3
    for mode in range(MODES):
        step = shift_ref[mode]
        above = col == row + step
        below = col == row - step
        mixing = mix_ref[mode]
        for kind in range(2):
            upper = occ_ref[mode] + (1.0 - kind)
            lower = occ_ref[mode] + float(kind)
            moved = jnp.where(above, upper, 0.0) + jnp.where(below, lower, 0.0)
            high, low = split(moved * mixing)
            high_ref[kind, POINTS * mode : POINTS * (mode + 1), :] = high
            low_ref[kind, POINTS * mode : POINTS * (mode + 1), :] = low


def compute_kernel(x_ref, weight_ref, high_ref, low_ref, out_ref):
    lane = lax.broadcasted_iota(jnp.int32, (POINTS, LANES), 1)
    rest = x_ref[pl.ds(24, POINTS, stride=ROWS), :]
    rest_out = jnp.zeros((POINTS, LANES), jnp.float32)
    for atom in range(ATOMS_HERE):
        tiles = [x_ref[pl.ds(8 * t + atom, POINTS, stride=ROWS), :] for t in range(3)]
        tiles.append(pltpu.roll(rest, (LANES - 16 * atom) % LANES, 1) if atom else rest)
        blocks = [tiles[0]]
        for b in range(1, 4):
            joined = jnp.where(lane < PAIRS - 28 * b, tiles[b], tiles[b - 1])
            blocks.append(pltpu.roll(joined, 28 * b, 1))
        rows = []
        for kind in range(2):
            x_high, x_low = split(jnp.concatenate(blocks[2 * kind : 2 * kind + 2], axis=1))
            table = high_ref[kind]
            moved = dot(
                jnp.concatenate([table, table], axis=1), jnp.concatenate([x_high, x_low], axis=0)
            ) + dot(low_ref[kind], x_high)
            y_high, y_low = split(moved)
            for part in range(2):
                lanes = slice(LANES * part, LANES * (part + 1))
                pieces = []
                for mode in range(MODES):
                    points = slice(POINTS * mode, POINTS * (mode + 1))
                    pieces += [y_high[points, lanes], y_low[points, lanes]]
                rows.append(jnp.concatenate(pieces, axis=1))
        result = dot(jnp.concatenate(rows, axis=0), weight_ref[atom])
        result = result[:, :LANES] + result[:, LANES:]
        turned = [result[:POINTS]]
        for b in range(1, 4):
            turned.append(
                pltpu.roll(result[POINTS * b : POINTS * (b + 1)], LANES - 28 * b, 1)
            )
        for t in range(3):
            out_ref[pl.ds(8 * t + atom, POINTS, stride=ROWS), :] = jnp.where(
                lane < PAIRS - 28 * t, turned[t], turned[t + 1]
            )
        tail = jnp.where(lane < 16, turned[3], 0.0)
        rest_out = rest_out + (pltpu.roll(tail, 16 * atom, 1) if atom else tail)
    out_ref[pl.ds(24, POINTS, stride=ROWS), :] = rest_out


def constants():
    pair = np.arange(LANES)
    valid = pair < PAIRS
    cols = np.zeros((LANES, 2 * LANES), np.float32)
    rows = np.zeros((2 * LANES, 16), np.float32)
    for k in range(ORB):
        cols[k, :LANES] = valid & (pair // ORB == k)
        cols[k, LANES:] = valid & (pair % ORB == k)
        rows[:LANES, k] = valid & (pair // ORB == k)
        rows[LANES:, k] = valid & (pair % ORB == k)
    return jnp.asarray(cols), jnp.asarray(rows)


def exchange(message):
    moved = lax.all_to_all(
        message.reshape(POINTS, ROWS, 1, LANES), AXES, split_axis=0, concat_axis=0, tiled=True
    )
    return moved.reshape(POINTS * ROWS, LANES)


def mixing(branch_weight, pair_branch):
    onehot = (
        pair_branch[:, :, None] == jnp.arange(branch_weight.shape[0], dtype=jnp.int32)
    ).astype(jnp.float32)
    return jnp.einsum("kjq,qm->mkj", onehot, branch_weight, precision=HIGHEST)


def on_device(green_blocks, couple_matrix, occupation, energy_shift, branch_weight, pair_branch):
    f32, bf16 = jnp.float32, jnp.bfloat16
    tiles = green_blocks.shape[4] // LANES
    message = pl.pallas_call(
        pack_kernel,
        grid=(tiles,),
        in_specs=[pl.BlockSpec((400, LANES), lambda i: (0, i))],
        out_specs=pl.BlockSpec((400, LANES), lambda i: (i, 0)),
        out_shape=jax.ShapeDtypeStruct((POINTS * ROWS, LANES), f32),
        scratch_shapes=[pltpu.VMEM((LANES, LANES), f32)],
        compiler_params=PARAMS,
        name="pack",
    )(green_blocks.reshape(400, tiles * LANES))
    received = exchange(message)

    table = jnp.tile(mixing(branch_weight, pair_branch) / pair_branch.shape[0], (1, 16, 16))
    turned = couple_matrix.reshape(MODES, ORB, ORB, ATOMS_HERE).transpose(3, 0, 2, 1)
    turned = jnp.pad(turned, ((0, 0), (0, 0), (0, 6), (0, LANES - ORB))).reshape(-1, LANES)
    cols, rows = constants()
    smem = pl.BlockSpec(memory_space=pltpu.SMEM)
    vmem = pl.BlockSpec(memory_space=pltpu.VMEM)
    weight, high, low = pl.pallas_call(
        prepare_kernel,
        in_specs=[smem, smem, vmem, vmem, vmem, vmem],
        out_specs=[vmem, vmem, vmem],
        out_shape=[
            jax.ShapeDtypeStruct((ATOMS_HERE, 2 * MODES * LANES, 2 * LANES), bf16),
            jax.ShapeDtypeStruct((2, MODES * POINTS, POINTS), bf16),
            jax.ShapeDtypeStruct((2, MODES * POINTS, POINTS), bf16),
        ],
        compiler_params=PARAMS,
        cost_estimate=pl.CostEstimate(flops=10**9, bytes_accessed=4 * 10**6, transcendentals=0),
        name="prepare",
    )(occupation, energy_shift, turned, table, cols, rows)

    result = pl.pallas_call(
        compute_kernel,
        in_specs=[vmem] * 4,
        out_specs=vmem,
        out_shape=jax.ShapeDtypeStruct((POINTS * ROWS, LANES), f32),
        compiler_params=PARAMS,
        name="compute",
    )(received, weight, high, low)
    returned = exchange(result)
    out = pl.pallas_call(
        unpack_kernel,
        grid=(tiles,),
        in_specs=[pl.BlockSpec((400, LANES), lambda i: (i, 0))],
        out_specs=pl.BlockSpec((400, LANES), lambda i: (0, i)),
        out_shape=jax.ShapeDtypeStruct((400, tiles * LANES), f32),
        scratch_shapes=[pltpu.VMEM((LANES, LANES), f32)],
        compiler_params=PARAMS,
        name="unpack",
    )(returned)
    return out.reshape(green_blocks.shape)


def solution(mesh):
    in_specs = (
        P(None, "energy", "momentum", None, None),
        P(None, None, ("energy", "momentum")),
        P(),
        P(),
        P(),
        P(),
    )
    out_specs = P(None, "energy", "momentum", None, None)
    return jax.shard_map(
        on_device, mesh=mesh, in_specs=in_specs, out_specs=out_specs, check_vma=False
    )
```

profile of v0, /device:TPU:1, one launch (start us, length us, event | category | flops | bytes accessed | tf_op | source)
XLA Modules:
  0.0 82.0 jit_solution(9752365943493670650)
XLA Ops:
  0.0 0.0 copy-start
  0.0 0.0 copy-start.2
  0.0 1.4 %copy-done.2 = f32[2,1,1,200,1024]{4,3,2,1,0:T(8,128)S(1)} copy-done((f32[2,1,1,200,1024]{4,3,2,1,0:T(8,128)S(1)}, f32[2,1,1,200,1024]{4,3,2,1,0:T(8,128)}, u32[]{:S(2)}) %copy-start.2) | copy-done | bytes 1638424
  1.4 4.3 %pack.1 = f32[3200,128]{1,0:T(8,128)} custom-call(f32[400,1024]{1,0:T(8,128)S(1)} %bitcast.22), custom_call_target="tpu_custom_call" | custom-call | tf_op jit(solution)/shard_map/pack/pallas_call | solution.py:171
  5.7 11.5 %all-to-all-start = ((f32[128,25,1,128]{3,2,1,0:T(1,128)}), f32[128,25,1,128]{3,2,1,0:T(1,128)S(1)}, u32[]{:S(2)}, u32[]{:S(2)}) async-start(f32[128,25,1,128]{3,2,1,0:T(1,128)} %bitcast.1), calls=%async_computation | async-start | bytes 3276800 | tf_op jit(solution)/shard_map/all_to_all | solution.py:155
  17.2 0.0 copy-done
  17.2 0.0 copy-done.8
  17.2 0.4 fusion
  17.6 0.0 copy-done.7
  17.7 0.1 reshape.32
  17.8 0.3 copy.20
  18.0 2.0 %tile.4 = f32[3,16,8,16,8]{4,3,2,1,0:T(8,128)} broadcast(f32[3,8,8]{2,1,0:T(8,128)S(1)} %copy.17), dimensions={0,2,4} | broadcast | bytes 197376 | tf_op jit(solution)/shard_map/tile | solution.py:183
  20.0 3.1 %tile.10.mix_ref = f32[3,128,128]{2,1,0:T(8,128)S(1)} reshape(f32[3,16,8,16,8]{4,3,2,1,0:T(8,128)} %tile.4) | data formatting | bytes 393216 | tf_op jit(solution)/shard_map/tile | solution.py:183
  23.1 0.0 copy-done.3
  23.2 0.0 copy-done.4
  23.2 0.0 copy-done.5
  23.2 0.0 copy-done.6
  23.2 4.3 %prepare.1 = (bf16[8,768,256]{2,1,0:T(8,128)(2,1)S(1)}, bf16[2,384,128]{2,1,0:T(8,128)(2,1)S(1)}, bf16[2,384,128]{2,1,0:T(8,128)(2,1)S(1)}) custom-call(f32[3]{0:T(128)S(1)} %copy-done.3, s32[3]{0:T(128)S(1)} %copy-done.4, f32[384,128]{1,0:T(8,128)S(1)} %bitcast.23, f32[3,128,128]{2,1,0:T(8,128)S(1)} %tile.10.mix_ref, f32[128,256]{1,0:T(8,128)S(1)} %copy-done.6, ...), custom_call_target="tpu_custom_call" | custom-call | flops 1000000000 | bytes 4000000 | tf_op jit(solution)/shard_map/prepare/pallas_call | solution.py:189
  27.5 0.0 copy-start.1
  27.5 1.6 %copy-done.1 = bf16[8,768,256]{2,1,0:T(8,128)(2,1)} copy-done((bf16[8,768,256]{2,1,0:T(8,128)(2,1)}, bf16[8,768,256]{2,1,0:T(8,128)(2,1)S(1)}, u32[]{:S(2)}) %copy-start.1) | copy-done | bytes 3145752
  29.1 13.7 %all-to-all-done = f32[128,25,1,128]{3,2,1,0:T(1,128)S(1)} async-done(((f32[128,25,1,128]{3,2,1,0:T(1,128)}), f32[128,25,1,128]{3,2,1,0:T(1,128)S(1)}, u32[]{:S(2)}, u32[]{:S(2)}) %all-to-all-start) | async-done | bytes 1638432 | tf_op jit(solution)/shard_map/all_to_all | solution.py:155
  42.8 5.9 %compute.1 = f32[3200,128]{1,0:T(8,128)S(1)} custom-call(f32[3200,128]{1,0:T(8,128)S(1)} %bitcast.20, bf16[8,768,256]{2,1,0:T(8,128)(2,1)} %copy-done.1, bf16[2,384,128]{2,1,0:T(8,128)(2,1)S(1)} %get-tuple-element.9.high_ref, bf16[2,384,128]{2,1,0:T(8,128)(2,1)S(1)} %get-tuple-element.10.low_ref), custom_call_target="tpu_custom_call" | custom-call | tf_op jit(solution)/shard_map/compute/pallas_call | solution.py:203
  48.8 29.7 %all_to_all.10 = f32[128,25,1,128]{3,2,1,0:T(1,128)S(1)} all-to-all(f32[128,25,1,128]{3,2,1,0:T(1,128)S(1)} %bitcast.21), channel_id=1, replica_groups=mesh['energy'=16,'momentum'=8] {'energy','momentum'}, dimensions={0} | all-to-all | bytes 3276800 | tf_op jit(solution)/shard_map/all_to_all | solution.py:155
  78.4 3.6 %unpack.1 = f32[400,1024]{1,0:T(8,128)} custom-call(f32[3200,128]{1,0:T(8,128)S(1)} %bitcast.19), custom_call_target="tpu_custom_call" | custom-call | tf_op jit(solution)/shard_map/unpack/pallas_call | solution.py:212
  (8 shorter events, 0.0 us)
Async XLA Ops:
  0.0 17.2 %copy-start = (f32[8,3]{0,1:T(4,128)S(1)}, f32[8,3]{0,1:T(4,128)}, u32[]{:S(2)}) copy-start(f32[8,3]{0,1:T(4,128)} %param.12) | copy-start | bytes 292
  0.0 1.4 %copy-start.2 = (f32[2,1,1,200,1024]{4,3,2,1,0:T(8,128)S(1)}, f32[2,1,1,200,1024]{4,3,2,1,0:T(8,128)}, u32[]{:S(2)}) copy-start(f32[2,1,1,200,1024]{4,3,2,1,0:T(8,128)} %param.8) | copy-start | bytes 4915204
  5.7 11.5 %copy-start.8 = (s32[8,8]{1,0:T(8,128)S(1)}, s32[8,8]{1,0:T(8,128)}, u32[]{:S(2)}) copy-start(s32[8,8]{1,0:T(8,128)} %param.13) | copy-start | bytes 772
  5.7 11.9 %copy-start.7 = (f32[3,100,8]{1,2,0:T(8,128)S(1)}, f32[3,100,8]{1,2,0:T(8,128)}, u32[]{:S(2)}) copy-start(f32[3,100,8]{1,2,0:T(8,128)} %param.9) | copy-start | bytes 28804
  5.7 37.1 %all-to-all-start = ((f32[128,25,1,128]{3,2,1,0:T(1,128)}), f32[128,25,1,128]{3,2,1,0:T(1,128)S(1)}, u32[]{:S(2)}, u32[]{:S(2)}) async-start(f32[128,25,1,128]{3,2,1,0:T(1,128)} %bitcast.1), calls=%async_computation | async-start | bytes 3276800 | tf_op jit(solution)/shard_map/all_to_all | solution.py:155
  20.0 3.2 %copy-start.3 = (f32[3]{0:T(128)S(1)}, f32[3]{0:T(128)}, u32[]{:S(2)}) copy-start(f32[3]{0:T(128)} %occ_ref.1) | copy-start | bytes 40
  20.0 3.2 %copy-start.4 = (s32[3]{0:T(128)S(1)}, s32[3]{0:T(128)}, u32[]{:S(2)}) copy-start(s32[3]{0:T(128)} %shift_ref.1) | copy-start | bytes 40
  20.0 3.2 %copy-start.5 = (f32[256,16]{1,0:T(8,128)S(1)}, f32[256,16]{1,0:T(8,128)}, u32[]{:S(2)}) copy-start(f32[256,16]{1,0:T(8,128)} %constant.11.clone.rows_ref) | copy-start | bytes 49156
  20.0 3.2 %copy-start.6 = (f32[128,256]{1,0:T(8,128)S(1)}, f32[128,256]{1,0:T(8,128)}, u32[]{:S(2)}) copy-start(f32[128,256]{1,0:T(8,128)} %constant.10.clone.cols_ref) | copy-start | bytes 393220
  27.5 1.6 %copy-start.1 = (bf16[8,768,256]{2,1,0:T(8,128)(2,1)}, bf16[8,768,256]{2,1,0:T(8,128)(2,1)S(1)}, u32[]{:S(2)}) copy-start(bf16[8,768,256]{2,1,0:T(8,128)(2,1)S(1)} %get-tuple-element.8.weight_ref) | copy-start | bytes 9437188
where the time goes:
time: 82.3 us; the launch traced here: 82 us
  blocking collectives  29.7 us (36%)
  Pallas kernels  18.1 us (22%)
  waiting for transfers between devices  13.7 us (17%)
  starting transfers between devices  11.5 us (14%)
  local copies, waits for them, and re-layouts  8.55 us (10%)
    all_to_all x1, blocking collectives, exchange(): lax.all_to_all(message.reshape(POINTS, ROWS, 1, LANES), AXES, split_axis=...  29.7 us
    all_to_all x1, waiting for transfers between devices, exchange(): lax.all_to_all(message.reshape(POINTS, ROWS, 1, LANES), AXES, split_axis=...  13.7 us
    all_to_all x1, starting transfers between devices, exchange(): lax.all_to_all(message.reshape(POINTS, ROWS, 1, LANES), AXES, split_axis=...  11.5 us
    pallas_call x1, Pallas kernels, on_device(): pl.pallas_call(compute_kernel, in_specs=[vmem] * 4, out_specs=vmem, out_s...  5.94 us
    another operation x2, local copies, waits for them, and re-layouts, on_device(): jnp.tile(mixing(branch_weight, pair_branch) / pair_branch.shape[0], (1, 1...  5.07 us
    pallas_call x1, Pallas kernels, on_device(): pl.pallas_call(prepare_kernel, in_specs=[smem, smem, vmem, vmem, vmem, vm...  4.31 us
    pallas_call x1, Pallas kernels, on_device(): pl.pallas_call(pack_kernel, grid=(tiles,), in_specs=[pl.BlockSpec((400, L...  4.26 us
    pallas_call x1, Pallas kernels, on_device(): pl.pallas_call(unpack_kernel, grid=(tiles,), in_specs=[pl.BlockSpec((400,...  3.59 us
  transfers between devices with their start and end apart: 1, of which 1 were waited for; matrix products, arithmetic and copies ran while one was open for 7% of the time, Pallas kernels for 5%

commit v1 on v0

v1 whole, which is shorter than its diff:
```python
import jax
import jax.numpy as jnp
import numpy as np
from jax import lax
from jax.experimental import pallas as pl
from jax.experimental.pallas import tpu as pltpu
from jax.sharding import PartitionSpec as P

ORB = 10
PAIRS = ORB * ORB
DEPTH = 112
LANES = 128
ATOMS_HERE = 8
ROWS = 25
POINTS = 128
MODES = 3
AXES = ("energy", "momentum")
HIGHEST = lax.Precision.HIGHEST
constrain = pltpu.with_memory_space_constraint
PARAMS = pltpu.CompilerParams(vmem_limit_bytes=32 * 1024 * 1024)


def split(value):
    high = value.astype(jnp.bfloat16)
    low = (value - high.astype(jnp.float32)).astype(jnp.bfloat16)
    return high, low


def dot(left, right):
    return lax.dot(left, right, preferred_element_type=jnp.float32)


def turn(value, lanes):
    return pltpu.roll(value, lanes % LANES, 1) if lanes % LANES else value


def pack_kernel(green_ref, out_ref, held_ref, rest_ref, sems):
    rest_copy = pltpu.make_async_copy(
        green_ref.at[pl.ds(384, 16), :], held_ref.at[pl.ds(384, 16), :], sems.at[2]
    )
    rest_copy.start()
    copies = []
    for half in range(2):
        place = (pl.ds(0, 384), pl.ds(512 * half, 512))
        copies.append(
            pltpu.make_async_copy(green_ref.at[place], held_ref.at[place], sems.at[half])
        )
        copies[half].start()
    rest_copy.wait()
    rest_ref[...] = jnp.concatenate(
        [held_ref[384:400, LANES * g : LANES * (g + 1)] for g in range(8)], axis=0
    ).T
    lane = lax.broadcasted_iota(jnp.int32, (16, LANES), 1)
    pieces = [rest_ref[pl.ds(atom, 16, stride=8), :] for atom in range(8)]
    for group in range(8):
        joined = None
        for atom in range(8):
            piece = turn(pieces[atom], 16 * (atom - group))
            joined = piece if joined is None else jnp.where(lane < 16 * atom, joined, piece)
        out_ref[pl.ds(400 * group + 24, 16, stride=ROWS), :] = joined
    for group in range(8):
        if group % 4 == 0:
            copies[group // 4].wait()
        for tile in range(3):
            turned = held_ref[
                LANES * tile : LANES * (tile + 1), LANES * group : LANES * (group + 1)
            ].T
            for owner in range(16):
                row = 400 * group + ROWS * owner + 8 * tile
                out_ref[row : row + 8, :] = turned[8 * owner : 8 * owner + 8, :]


def unpack_kernel(in_ref, out_ref, held_ref, rest_ref, sems):
    lane = lax.broadcasted_iota(jnp.int32, (16, LANES), 1)
    pieces = [in_ref[pl.ds(400 * group + 24, 16, stride=ROWS), :] for group in range(8)]
    for atom in range(8):
        joined = None
        for group in range(8):
            piece = turn(pieces[group], 16 * (group - atom))
            joined = piece if joined is None else jnp.where(lane < 16 * group, joined, piece)
        rest_ref[pl.ds(atom, 16, stride=8), :] = joined
    turned = rest_ref[...].T
    for group in range(8):
        held_ref[384:400, LANES * group : LANES * (group + 1)] = turned[
            16 * group : 16 * group + 16, :
        ]
    copies = [
        pltpu.make_async_copy(
            held_ref.at[pl.ds(384, 16), :], out_ref.at[pl.ds(384, 16), :], sems.at[8]
        )
    ]
    copies[0].start()
    for group in range(8):
        for tile in range(3):
            rows = [400 * group + ROWS * owner + 8 * tile for owner in range(16)]
            held_ref[
                LANES * tile : LANES * (tile + 1), LANES * group : LANES * (group + 1)
            ] = jnp.concatenate([in_ref[row : row + 8, :] for row in rows], axis=0).T
        place = (pl.ds(0, 384), pl.ds(LANES * group, LANES))
        copies.append(
            pltpu.make_async_copy(held_ref.at[place], out_ref.at[place], sems.at[group])
        )
        copies[-1].start()
    for copy in copies:
        copy.wait()


def prepare_kernel(
    occ_ref, shift_ref, couple_ref, mix_ref, cols_ref, rows_ref, out_ref, high_ref, low_ref
):
    spread = lax.dot(
        couple_ref[...], cols_ref[...], precision=HIGHEST, preferred_element_type=jnp.float32
    )
    for index in range(ATOMS_HERE * MODES):
        part = spread[16 * index : 16 * index + 16, :]
        first = lax.dot(
            rows_ref[:LANES, :], part[:, :LANES], precision=HIGHEST,
            preferred_element_type=jnp.float32,
        )
        second = lax.dot(
            rows_ref[LANES:, :], part[:, LANES:], precision=HIGHEST,
            preferred_element_type=jnp.float32,
        )
        high, low = split(first * second)
        out_ref[index, :, :LANES] = high[:DEPTH]
        out_ref[index, :, LANES:] = low[:DEPTH]
    row = lax.broadcasted_iota(jnp.int32, (POINTS, POINTS), 0) >> 3
    col = lax.broadcasted_iota(jnp.int32, (POINTS, POINTS), 1) >> 3
    for mode in range(MODES):
        step = shift_ref[mode]
        above = col == row + step
        below = col == row - step
        mixing = mix_ref[mode]
        for kind in range(2):
            upper = occ_ref[mode] + (1.0 - kind)
            lower = occ_ref[mode] + float(kind)
            moved = jnp.where(above, upper, 0.0) + jnp.where(below, lower, 0.0)
            high, low = split(moved * mixing)
            high_ref[kind, POINTS * mode : POINTS * (mode + 1), :] = high
            low_ref[kind, POINTS * mode : POINTS * (mode + 1), :] = low


def compute_kernel(x_ref, weight_ref, high_ref, low_ref, out_ref):
    lane = lax.broadcasted_iota(jnp.int32, (POINTS, LANES), 1)
    rest = x_ref[pl.ds(24, POINTS, stride=ROWS), :]
    rest_out = jnp.zeros((POINTS, LANES), jnp.float32)
    blank = jnp.zeros((LANES - DEPTH, 2 * LANES), jnp.bfloat16)
    for atom in range(ATOMS_HERE):
        tiles = [x_ref[pl.ds(8 * t + atom, POINTS, stride=ROWS), :] for t in range(3)]
        tiles.append(turn(rest, -16 * atom))
        blocks = [tiles[0]]
        for b in range(1, 4):
            joined = jnp.where(lane < PAIRS - 28 * b, tiles[b], tiles[b - 1])
            blocks.append(turn(joined, 28 * b))
        rows = []
        for kind in range(2):
            x_high, x_low = split(jnp.concatenate(blocks[2 * kind : 2 * kind + 2], axis=1))
            table = high_ref[kind]
            moved = dot(
                jnp.concatenate([table, table], axis=1), jnp.concatenate([x_high, x_low], axis=0)
            ) + dot(low_ref[kind], x_high)
            y_high, y_low = split(moved)
            for part in range(2):
                lanes = slice(LANES * part, LANES * (part + 1))
                pieces = []
                for mode in range(MODES):
                    points = slice(POINTS * mode, POINTS * (mode + 1))
                    pieces += [y_high[points, lanes], y_low[points, lanes]]
                rows.append(jnp.concatenate(pieces, axis=1))
        weights = []
        for mode in range(MODES):
            both = jnp.concatenate([weight_ref[MODES * atom + mode], blank], axis=0)
            weights += [both, jnp.concatenate([both[:, :LANES], jnp.zeros_like(both[:, LANES:])], axis=1)]
        result = dot(jnp.concatenate(rows, axis=0), jnp.concatenate(weights, axis=0))
        result = result[:, :LANES] + result[:, LANES:]
        turned = [turn(result[POINTS * b : POINTS * (b + 1)], -28 * b) for b in range(4)]
        for t in range(3):
            out_ref[pl.ds(8 * t + atom, POINTS, stride=ROWS), :] = jnp.where(
                lane < PAIRS - 28 * t, turned[t], turned[t + 1]
            )
        tail = jnp.where(lane < 16, turned[3], 0.0)
        rest_out = rest_out + turn(tail, 16 * atom)
    out_ref[pl.ds(24, POINTS, stride=ROWS), :] = rest_out


def constants():
    pair = np.arange(LANES)
    valid = pair < PAIRS
    cols = np.zeros((LANES, 2 * LANES), np.float32)
    rows = np.zeros((2 * LANES, 16), np.float32)
    for k in range(ORB):
        cols[k, :LANES] = valid & (pair // ORB == k)
        cols[k, LANES:] = valid & (pair % ORB == k)
        rows[:LANES, k] = valid & (pair // ORB == k)
        rows[LANES:, k] = valid & (pair % ORB == k)
    return jnp.asarray(cols), jnp.asarray(rows)


def exchange(message):
    moved = lax.all_to_all(
        message.reshape(POINTS, ROWS, 1, LANES), AXES, split_axis=0, concat_axis=0, tiled=True
    )
    return moved.reshape(POINTS * ROWS, LANES)


def mixing(branch_weight, pair_branch):
    onehot = (
        pair_branch[:, :, None] == jnp.arange(branch_weight.shape[0], dtype=jnp.int32)
    ).astype(jnp.float32)
    return jnp.einsum("kjq,qm->mkj", onehot, branch_weight, precision=HIGHEST)


def on_device(green_blocks, couple_matrix, occupation, energy_shift, branch_weight, pair_branch):
    f32, bf16 = jnp.float32, jnp.bfloat16
    smem = pl.BlockSpec(memory_space=pltpu.SMEM)
    vmem = pl.BlockSpec(memory_space=pltpu.VMEM)
    hbm = pl.BlockSpec(memory_space=pltpu.HBM)
    tiles = green_blocks.shape[4] // LANES
    message = pl.pallas_call(
        pack_kernel,
        in_specs=[hbm],
        out_specs=vmem,
        out_shape=pltpu.VMEM((POINTS * ROWS, LANES), f32),
        scratch_shapes=[
            pltpu.VMEM((400, tiles * LANES), f32),
            pltpu.VMEM((LANES, LANES), f32),
            pltpu.SemaphoreType.DMA((3,)),
        ],
        compiler_params=PARAMS,
        name="pack",
    )(constrain(green_blocks.reshape(400, tiles * LANES), pltpu.HBM))
    received = exchange(message)

    table = jnp.tile(mixing(branch_weight, pair_branch) / pair_branch.shape[0], (1, 16, 16))
    turned = couple_matrix.reshape(MODES, ORB, ORB, ATOMS_HERE).transpose(3, 0, 2, 1)
    turned = jnp.pad(turned, ((0, 0), (0, 0), (0, 6), (0, LANES - ORB))).reshape(-1, LANES)
    cols, rows = constants()
    weight, high, low = pl.pallas_call(
        prepare_kernel,
        in_specs=[smem, smem, vmem, vmem, vmem, vmem],
        out_specs=[vmem, vmem, vmem],
        out_shape=[
            pltpu.VMEM((ATOMS_HERE * MODES, DEPTH, 2 * LANES), bf16),
            pltpu.VMEM((2, MODES * POINTS, POINTS), bf16),
            pltpu.VMEM((2, MODES * POINTS, POINTS), bf16),
        ],
        compiler_params=PARAMS,
        cost_estimate=pl.CostEstimate(flops=10**9, bytes_accessed=4 * 10**6, transcendentals=0),
        name="prepare",
    )(occupation, energy_shift, turned, table, cols, rows)

    result = pl.pallas_call(
        compute_kernel,
        in_specs=[vmem] * 4,
        out_specs=vmem,
        out_shape=pltpu.VMEM((POINTS * ROWS, LANES), f32),
        compiler_params=PARAMS,
        name="compute",
    )(*(constrain(value, pltpu.VMEM) for value in (received, weight, high, low)))
    returned = exchange(result)
    out = pl.pallas_call(
        unpack_kernel,
        in_specs=[vmem],
        out_specs=hbm,
        out_shape=pltpu.HBM((400, tiles * LANES), f32),
        scratch_shapes=[
            pltpu.VMEM((400, tiles * LANES), f32),
            pltpu.VMEM((LANES, LANES), f32),
            pltpu.SemaphoreType.DMA((9,)),
        ],
        compiler_params=PARAMS,
        name="unpack",
    )(constrain(returned, pltpu.VMEM))
    return out.reshape(green_blocks.shape)


def solution(mesh):
    in_specs = (
        P(None, "energy", "momentum", None, None),
        P(None, None, ("energy", "momentum")),
        P(),
        P(),
        P(),
        P(),
    )
    out_specs = P(None, "energy", "momentum", None, None)
    return jax.shard_map(
        on_device, mesh=mesh, in_specs=in_specs, out_specs=out_specs, check_vma=False
    )
```

time: 82.3 us -> 75.6 us (0.919)
  Pallas kernels: 18.1 us -> 12.7 us
    pallas_call x2, Pallas kernels: 7.85 us -> 4.46 us  [the longest x1 2.91 us: on_device(): pl.pallas_call(pack_kernel, in_specs=[hbm], out_specs=vmem, out_shape=plt...]
    pallas_call x1, Pallas kernels: 5.94 us -> 4.07 us  [on_device(): pl.pallas_call(compute_kernel, in_specs=[vmem] * 4, out_specs=vmem, out_s...]
    unnamed x19 -> x17, local copies, waits for them, and re-layouts: 3.35 us -> 2.11 us
  transfers between devices with their start and end apart: 1 -> 1, of which waited for: 1 -> 1; matrix products, arithmetic and copies ran while one was open for 7% -> 9% of each run, Pallas kernels for 5% -> 6%
where the time goes in v1:
time: 75.6 us; the launch traced here: 75.4 us
  blocking collectives  29.7 us (39%)
  waiting for transfers between devices  12.9 us (17%)
  Pallas kernels  12.7 us (17%)
  starting transfers between devices  11.5 us (15%)
  local copies, waits for them, and re-layouts  7.99 us (11%)
    all_to_all x1, blocking collectives, exchange(): lax.all_to_all(message.reshape(POINTS, ROWS, 1, LANES), AXES, split_axis=...  29.7 us
    all_to_all x1, waiting for transfers between devices, exchange(): lax.all_to_all(message.reshape(POINTS, ROWS, 1, LANES), AXES, split_axis=...  12.9 us
    all_to_all x1, starting transfers between devices, exchange(): lax.all_to_all(message.reshape(POINTS, ROWS, 1, LANES), AXES, split_axis=...  11.5 us
    another operation x2, local copies, waits for them, and re-layouts, on_device(): jnp.tile(mixing(branch_weight, pair_branch) / pair_branch.shape[0], (1, 1...  5.76 us
    pallas_call x1, Pallas kernels, on_device(): pl.pallas_call(prepare_kernel, in_specs=[smem, smem, vmem, vmem, vmem, vm...  4.2 us
    pallas_call x1, Pallas kernels, on_device(): pl.pallas_call(compute_kernel, in_specs=[vmem] * 4, out_specs=vmem, out_s...  4.07 us
    pallas_call x1, Pallas kernels, on_device(): pl.pallas_call(pack_kernel, in_specs=[hbm], out_specs=vmem, out_shape=plt...  2.91 us
    unnamed x17, local copies, waits for them, and re-layouts  2.11 us
  transfers between devices with their start and end apart: 1, of which 1 were waited for; matrix products, arithmetic and copies ran while one was open for 9% of the time, Pallas kernels for 6%

profile of v1, /device:TPU:1, one launch (start us, length us, event | category | flops | bytes accessed | tf_op | source)
XLA Modules:
  0.0 75.4 jit_solution(7468575272148376795)
XLA Ops:
  0.0 0.0 copy-start
  0.0 2.9 %pack.1 = f32[3200,128]{1,0:T(8,128)} custom-call(f32[400,1024]{1,0:T(8,128)} %bitcast.23), custom_call_target="tpu_custom_call" | custom-call | tf_op jit(solution)/shard_map/pack/pallas_call | solution.py:219
  2.9 0.0 copy-start.7
  2.9 11.5 %all-to-all-start = ((f32[128,25,1,128]{3,2,1,0:T(1,128)}), f32[128,25,1,128]{3,2,1,0:T(1,128)S(1)}, u32[]{:S(2)}, u32[]{:S(2)}) async-start(f32[128,25,1,128]{3,2,1,0:T(1,128)} %bitcast.1), calls=%async_computation | async-start | bytes 3276800 | tf_op jit(solution)/shard_map/all_to_all | solution.py:200
  14.4 0.0 copy-done
  14.5 0.0 copy-done.7
  14.5 0.4 fusion
  14.9 2.0 %tile.4 = f32[3,16,8,16,8]{4,3,2,1,0:T(8,128)} broadcast(f32[3,8,8]{2,1,0:T(8,128)S(1)} %copy.17), dimensions={0,2,4} | broadcast | bytes 197376 | tf_op jit(solution)/shard_map/tile | solution.py:234
  16.9 0.0 copy-start.6
  16.9 3.8 %tile.10.mix_ref = f32[3,128,128]{2,1,0:T(8,128)} reshape(f32[3,16,8,16,8]{4,3,2,1,0:T(8,128)} %tile.4) | data formatting | bytes 393216 | tf_op jit(solution)/shard_map/tile | solution.py:234
  20.6 0.0 copy-done.6
  20.6 0.1 reshape.32
  20.8 0.3 copy.20
  21.0 0.0 copy-done.2
  21.0 0.0 copy-done.3
  21.1 0.0 copy-done.4
  21.1 0.0 copy-start.1
  21.1 0.9 %copy-done.1 = f32[3,128,128]{2,1,0:T(8,128)S(1)} copy-done((f32[3,128,128]{2,1,0:T(8,128)S(1)}, f32[3,128,128]{2,1,0:T(8,128)}, u32[]{:S(2)}) %copy-start.1) | copy-done | bytes 196632
  22.0 0.9 %copy-done.5 = f32[256,16]{1,0:T(8,128)S(1)} copy-done((f32[256,16]{1,0:T(8,128)S(1)}, f32[256,16]{1,0:T(8,128)}, u32[]{:S(2)}) %copy-start.5) | copy-done | bytes 16408
  22.9 4.2 %prepare.1 = (bf16[24,112,256]{2,1,0:T(8,128)(2,1)S(1)}, bf16[2,384,128]{2,1,0:T(8,128)(2,1)S(1)}, bf16[2,384,128]{2,1,0:T(8,128)(2,1)S(1)}) custom-call(f32[3]{0:T(128)S(1)} %copy-done.2, s32[3]{0:T(128)S(1)} %copy-done.3, f32[384,128]{1,0:T(8,128)S(1)} %bitcast.22, f32[3,128,128]{2,1,0:T(8,128)S(1)} %copy-done.1, f32[128,256]{1,0:T(8,128)S(1)} %copy-done.4, ...), custom_call_target="tpu_custom_call" | custom-call | flops 1000000000 | bytes 4000000 | tf_op jit(solution)/shard_map/prepare/pallas_call | solution.py:238
  27.1 12.9 %all-to-all-done = f32[128,25,1,128]{3,2,1,0:T(1,128)S(1)} async-done(((f32[128,25,1,128]{3,2,1,0:T(1,128)}), f32[128,25,1,128]{3,2,1,0:T(1,128)S(1)}, u32[]{:S(2)}, u32[]{:S(2)}) %all-to-all-start) | async-done | bytes 1638432 | tf_op jit(solution)/shard_map/all_to_all | solution.py:200
  40.0 4.1 %compute.1 = f32[3200,128]{1,0:T(8,128)S(1)} custom-call(f32[3200,128]{1,0:T(8,128)S(1)} %bitcast.19, bf16[24,112,256]{2,1,0:T(8,128)(2,1)S(1)} %get-tuple-element.8.weight_ref, bf16[2,384,128]{2,1,0:T(8,128)(2,1)S(1)} %get-tuple-element.9.high_ref, bf16[2,384,128]{2,1,0:T(8,128)(2,1)S(1)} %get-tuple-element.10.low_ref), custom_call_target="tpu_custom_call" | custom-call | tf_op jit(solution)/shard_map/compute/pallas_call | solution.py:252
  44.1 29.7 %all_to_all.10 = f32[128,25,1,128]{3,2,1,0:T(1,128)S(1)} all-to-all(f32[128,25,1,128]{3,2,1,0:T(1,128)S(1)} %bitcast.20), channel_id=1, replica_groups=mesh['energy'=16,'momentum'=8] {'energy','momentum'}, dimensions={0} | all-to-all | bytes 3276800 | tf_op jit(solution)/shard_map/all_to_all | solution.py:200
  73.8 1.5 %unpack.1 = f32[400,1024]{1,0:T(8,128)} custom-call(f32[3200,128]{1,0:T(8,128)S(1)} %bitcast.21), custom_call_target="tpu_custom_call" | custom-call | tf_op jit(solution)/shard_map/unpack/pallas_call | solution.py:261
  (6 shorter events, 0.0 us)
Async XLA Ops:
  0.0 14.4 %copy-start = (f32[8,3]{0,1:T(4,128)S(1)}, f32[8,3]{0,1:T(4,128)}, u32[]{:S(2)}) copy-start(f32[8,3]{0,1:T(4,128)} %param.12) | copy-start | bytes 292
  2.9 11.5 %copy-start.7 = (s32[8,8]{1,0:T(8,128)S(1)}, s32[8,8]{1,0:T(8,128)}, u32[]{:S(2)}) copy-start(s32[8,8]{1,0:T(8,128)} %param.13) | copy-start | bytes 772
  2.9 37.1 %all-to-all-start = ((f32[128,25,1,128]{3,2,1,0:T(1,128)}), f32[128,25,1,128]{3,2,1,0:T(1,128)S(1)}, u32[]{:S(2)}, u32[]{:S(2)}) async-start(f32[128,25,1,128]{3,2,1,0:T(1,128)} %bitcast.1), calls=%async_computation | async-start | bytes 3276800 | tf_op jit(solution)/shard_map/all_to_all | solution.py:200
  16.9 3.8 %copy-start.6 = (f32[3,100,8]{1,2,0:T(8,128)S(1)}, f32[3,100,8]{1,2,0:T(8,128)}, u32[]{:S(2)}) copy-start(f32[3,100,8]{1,2,0:T(8,128)} %param.9) | copy-start | bytes 28804
  16.9 4.2 %copy-start.2 = (f32[3]{0:T(128)S(1)}, f32[3]{0:T(128)}, u32[]{:S(2)}) copy-start(f32[3]{0:T(128)} %occ_ref.1) | copy-start | bytes 40
  16.9 4.2 %copy-start.3 = (s32[3]{0:T(128)S(1)}, s32[3]{0:T(128)}, u32[]{:S(2)}) copy-start(s32[3]{0:T(128)} %shift_ref.1) | copy-start | bytes 40
  16.9 4.2 %copy-start.4 = (f32[128,256]{1,0:T(8,128)S(1)}, f32[128,256]{1,0:T(8,128)}, u32[]{:S(2)}) copy-start(f32[128,256]{1,0:T(8,128)} %constant.10.clone.cols_ref) | copy-start | bytes 393220
  21.1 0.9 %copy-start.1 = (f32[3,128,128]{2,1,0:T(8,128)S(1)}, f32[3,128,128]{2,1,0:T(8,128)}, u32[]{:S(2)}) copy-start(f32[3,128,128]{2,1,0:T(8,128)} %tile.10.mix_ref) | copy-start | bytes 589828
  22.0 0.9 %copy-start.5 = (f32[256,16]{1,0:T(8,128)S(1)}, f32[256,16]{1,0:T(8,128)}, u32[]{:S(2)}) copy-start(f32[256,16]{1,0:T(8,128)} %constant.11.clone.rows_ref) | copy-start | bytes 49156

commit v2 on v1

--- a/solution.py
+++ b/solution.py
@@ -34,7 +34,7 @@
     return pltpu.roll(value, lanes % LANES, 1) if lanes % LANES else value
 
 
-def pack_kernel(green_ref, out_ref, held_ref, rest_ref, sems):
+def pack_kernel(green_ref, out_ref, held_ref, message_ref, rest_ref, sems, out_sems):
     rest_copy = pltpu.make_async_copy(
         green_ref.at[pl.ds(384, 16), :], held_ref.at[pl.ds(384, 16), :], sems.at[2]
     )
@@ -57,7 +57,7 @@
         for atom in range(8):
             piece = turn(pieces[atom], 16 * (atom - group))
             joined = piece if joined is None else jnp.where(lane < 16 * atom, joined, piece)
-        out_ref[pl.ds(400 * group + 24, 16, stride=ROWS), :] = joined
+        message_ref[pl.ds(400 * group + 24, 16, stride=ROWS), :] = joined
     for group in range(8):
         if group % 4 == 0:
             copies[group // 4].wait()
@@ -67,7 +67,14 @@
             ].T
             for owner in range(16):
                 row = 400 * group + ROWS * owner + 8 * tile
-                out_ref[row : row + 8, :] = turned[8 * owner : 8 * owner + 8, :]
+                message_ref[row : row + 8, :] = turned[8 * owner : 8 * owner + 8, :]
+        place = pl.ds(400 * group, 400)
+        copies.append(
+            pltpu.make_async_copy(message_ref.at[place], out_ref.at[place], out_sems.at[group])
+        )
+        copies[-1].start()
+    for copy in copies[2:]:
+        copy.wait()
 
 
 def unpack_kernel(in_ref, out_ref, held_ref, rest_ref, sems):
@@ -143,43 +150,57 @@
 def compute_kernel(x_ref, weight_ref, high_ref, low_ref, out_ref):
     lane = lax.broadcasted_iota(jnp.int32, (POINTS, LANES), 1)
     rest = x_ref[pl.ds(24, POINTS, stride=ROWS), :]
-    rest_out = jnp.zeros((POINTS, LANES), jnp.float32)
     blank = jnp.zeros((LANES - DEPTH, 2 * LANES), jnp.bfloat16)
-    for atom in range(ATOMS_HERE):
+
+    def shifted(atom):
         tiles = [x_ref[pl.ds(8 * t + atom, POINTS, stride=ROWS), :] for t in range(3)]
         tiles.append(turn(rest, -16 * atom))
         blocks = [tiles[0]]
         for b in range(1, 4):
             joined = jnp.where(lane < PAIRS - 28 * b, tiles[b], tiles[b - 1])
             blocks.append(turn(joined, 28 * b))
-        rows = []
+        parts = []
         for kind in range(2):
             x_high, x_low = split(jnp.concatenate(blocks[2 * kind : 2 * kind + 2], axis=1))
             table = high_ref[kind]
             moved = dot(
                 jnp.concatenate([table, table], axis=1), jnp.concatenate([x_high, x_low], axis=0)
             ) + dot(low_ref[kind], x_high)
-            y_high, y_low = split(moved)
+            parts.append(split(moved))
+        return parts
+
+    def sandwiched(atom, parts):
+        rows = []
+        for high, low in parts:
             for part in range(2):
                 lanes = slice(LANES * part, LANES * (part + 1))
                 pieces = []
                 for mode in range(MODES):
                     points = slice(POINTS * mode, POINTS * (mode + 1))
-                    pieces += [y_high[points, lanes], y_low[points, lanes]]
+                    pieces += [high[points, lanes], low[points, lanes]]
                 rows.append(jnp.concatenate(pieces, axis=1))
         weights = []
         for mode in range(MODES):
             both = jnp.concatenate([weight_ref[MODES * atom + mode], blank], axis=0)
-            weights += [both, jnp.concatenate([both[:, :LANES], jnp.zeros_like(both[:, LANES:])], axis=1)]
+            weights += [
+                both,
+                jnp.concatenate([both[:, :LANES], jnp.zeros_like(both[:, LANES:])], axis=1),
+            ]
         result = dot(jnp.concatenate(rows, axis=0), jnp.concatenate(weights, axis=0))
-        result = result[:, :LANES] + result[:, LANES:]
+        return result[:, :LANES] + result[:, LANES:]
+
+    rest_out = jnp.zeros((POINTS, LANES), jnp.float32)
+    parts = shifted(0)
+    for atom in range(ATOMS_HERE):
+        following = shifted(atom + 1) if atom + 1 < ATOMS_HERE else None
+        result = sandwiched(atom, parts)
         turned = [turn(result[POINTS * b : POINTS * (b + 1)], -28 * b) for b in range(4)]
         for t in range(3):
             out_ref[pl.ds(8 * t + atom, POINTS, stride=ROWS), :] = jnp.where(
                 lane < PAIRS - 28 * t, turned[t], turned[t + 1]
             )
-        tail = jnp.where(lane < 16, turned[3], 0.0)
-        rest_out = rest_out + turn(tail, 16 * atom)
+        rest_out = rest_out + turn(jnp.where(lane < 16, turned[3], 0.0), 16 * atom)
+        parts = following
     out_ref[pl.ds(24, POINTS, stride=ROWS), :] = rest_out
 
 
@@ -219,12 +240,14 @@
     message = pl.pallas_call(
         pack_kernel,
         in_specs=[hbm],
-        out_specs=vmem,
-        out_shape=pltpu.VMEM((POINTS * ROWS, LANES), f32),
+        out_specs=hbm,
+        out_shape=pltpu.HBM((POINTS * ROWS, LANES), f32),
         scratch_shapes=[
             pltpu.VMEM((400, tiles * LANES), f32),
+            pltpu.VMEM((POINTS * ROWS, LANES), f32),
             pltpu.VMEM((LANES, LANES), f32),
             pltpu.SemaphoreType.DMA((3,)),
+            pltpu.SemaphoreType.DMA((8,)),
         ],
         compiler_params=PARAMS,
         name="pack",

time: 75.6 us -> 74.9 us (level)
  no operation moved by 1% of the time
where the time goes in v2:
time: 74.9 us; the launch traced here: 74.6 us
  blocking collectives  29.7 us (40%)
  waiting for transfers between devices  12.9 us (17%)
  Pallas kernels  12 us (16%)
  starting transfers between devices  11.5 us (15%)
  local copies, waits for them, and re-layouts  7.99 us (11%)
    all_to_all x1, blocking collectives, exchange(): lax.all_to_all(message.reshape(POINTS, ROWS, 1, LANES), AXES, split_axis=...  29.7 us
    all_to_all x1, waiting for transfers between devices, exchange(): lax.all_to_all(message.reshape(POINTS, ROWS, 1, LANES), AXES, split_axis=...  12.9 us
    all_to_all x1, starting transfers between devices, exchange(): lax.all_to_all(message.reshape(POINTS, ROWS, 1, LANES), AXES, split_axis=...  11.5 us
    another operation x2, local copies, waits for them, and re-layouts, on_device(): jnp.tile(mixing(branch_weight, pair_branch) / pair_branch.shape[0], (1, 1...  5.76 us
    pallas_call x1, Pallas kernels, on_device(): pl.pallas_call(prepare_kernel, in_specs=[smem, smem, vmem, vmem, vmem, vm...  4.2 us
    pallas_call x1, Pallas kernels, on_device(): pl.pallas_call(compute_kernel, in_specs=[vmem] * 4, out_specs=vmem, out_s...  3.71 us
    pallas_call x1, Pallas kernels, on_device(): pl.pallas_call(pack_kernel, in_specs=[hbm], out_specs=hbm, out_shape=pltp...  2.57 us
    unnamed x17, local copies, waits for them, and re-layouts  2.11 us
  transfers between devices with their start and end apart: 1, of which 1 were waited for; matrix products, arithmetic and copies ran while one was open for 9% of the time, Pallas kernels for 6%

profile of v2, /device:TPU:1, one launch (start us, length us, event | category | flops | bytes accessed | tf_op | source)
XLA Modules:
  0.0 74.6 jit_solution(1021054391111526360)
XLA Ops:
  0.0 0.0 copy-start
  0.0 2.6 %pack.1 = f32[3200,128]{1,0:T(8,128)} custom-call(f32[400,1024]{1,0:T(8,128)} %bitcast.24), custom_call_target="tpu_custom_call" | custom-call | tf_op jit(solution)/shard_map/pack/pallas_call | solution.py:240
  2.6 0.0 copy-start.7
  2.6 11.5 %all-to-all-start = ((f32[128,25,1,128]{3,2,1,0:T(1,128)}), f32[128,25,1,128]{3,2,1,0:T(1,128)S(1)}, u32[]{:S(2)}, u32[]{:S(2)}) async-start(f32[128,25,1,128]{3,2,1,0:T(1,128)} %bitcast.23), calls=%async_computation | async-start | bytes 3276800 | tf_op jit(solution)/shard_map/all_to_all | solution.py:221
  14.1 0.0 copy-done
  14.1 0.0 copy-done.7
  14.1 0.4 fusion
  14.5 2.0 %tile.4 = f32[3,16,8,16,8]{4,3,2,1,0:T(8,128)} broadcast(f32[3,8,8]{2,1,0:T(8,128)S(1)} %copy.17), dimensions={0,2,4} | broadcast | bytes 197376 | tf_op jit(solution)/shard_map/tile | solution.py:257
  16.5 0.0 copy-start.6
  16.5 3.8 %tile.10.mix_ref = f32[3,128,128]{2,1,0:T(8,128)} reshape(f32[3,16,8,16,8]{4,3,2,1,0:T(8,128)} %tile.4) | data formatting | bytes 393216 | tf_op jit(solution)/shard_map/tile | solution.py:257
  20.3 0.0 copy-done.6
  20.3 0.1 reshape.32
  20.4 0.3 copy.20
  20.7 0.0 copy-done.2
  20.7 0.0 copy-done.3
  20.7 0.0 copy-done.4
  20.7 0.0 copy-start.1
  20.7 0.9 %copy-done.1 = f32[3,128,128]{2,1,0:T(8,128)S(1)} copy-done((f32[3,128,128]{2,1,0:T(8,128)S(1)}, f32[3,128,128]{2,1,0:T(8,128)}, u32[]{:S(2)}) %copy-start.1) | copy-done | bytes 196632
  21.6 0.9 %copy-done.5 = f32[256,16]{1,0:T(8,128)S(1)} copy-done((f32[256,16]{1,0:T(8,128)S(1)}, f32[256,16]{1,0:T(8,128)}, u32[]{:S(2)}) %copy-start.5) | copy-done | bytes 16408
  22.6 4.2 %prepare.1 = (bf16[24,112,256]{2,1,0:T(8,128)(2,1)S(1)}, bf16[2,384,128]{2,1,0:T(8,128)(2,1)S(1)}, bf16[2,384,128]{2,1,0:T(8,128)(2,1)S(1)}) custom-call(f32[3]{0:T(128)S(1)} %copy-done.2, s32[3]{0:T(128)S(1)} %copy-done.3, f32[384,128]{1,0:T(8,128)S(1)} %bitcast.22, f32[3,128,128]{2,1,0:T(8,128)S(1)} %copy-done.1, f32[128,256]{1,0:T(8,128)S(1)} %copy-done.4, ...), custom_call_target="tpu_custom_call" | custom-call | flops 1000000000 | bytes 4000000 | tf_op jit(solution)/shard_map/prepare/pallas_call | solution.py:261
  26.8 12.9 %all-to-all-done = f32[128,25,1,128]{3,2,1,0:T(1,128)S(1)} async-done(((f32[128,25,1,128]{3,2,1,0:T(1,128)}), f32[128,25,1,128]{3,2,1,0:T(1,128)S(1)}, u32[]{:S(2)}, u32[]{:S(2)}) %all-to-all-start) | async-done | bytes 1638432 | tf_op jit(solution)/shard_map/all_to_all | solution.py:221
  39.7 3.7 %compute.1 = f32[3200,128]{1,0:T(8,128)S(1)} custom-call(f32[3200,128]{1,0:T(8,128)S(1)} %bitcast.19, bf16[24,112,256]{2,1,0:T(8,128)(2,1)S(1)} %get-tuple-element.8.weight_ref, bf16[2,384,128]{2,1,0:T(8,128)(2,1)S(1)} %get-tuple-element.9.high_ref, bf16[2,384,128]{2,1,0:T(8,128)(2,1)S(1)} %get-tuple-element.10.low_ref), custom_call_target="tpu_custom_call" | custom-call | tf_op jit(solution)/shard_map/compute/pallas_call | solution.py:275
  43.4 29.7 %all_to_all.10 = f32[128,25,1,128]{3,2,1,0:T(1,128)S(1)} all-to-all(f32[128,25,1,128]{3,2,1,0:T(1,128)S(1)} %bitcast.20), channel_id=1, replica_groups=mesh['energy'=16,'momentum'=8] {'energy','momentum'}, dimensions={0} | all-to-all | bytes 3276800 | tf_op jit(solution)/shard_map/all_to_all | solution.py:221
  73.1 1.5 %unpack.1 = f32[400,1024]{1,0:T(8,128)} custom-call(f32[3200,128]{1,0:T(8,128)S(1)} %bitcast.21), custom_call_target="tpu_custom_call" | custom-call | tf_op jit(solution)/shard_map/unpack/pallas_call | solution.py:284
  (6 shorter events, 0.0 us)
Async XLA Ops:
  0.0 14.1 %copy-start = (f32[8,3]{0,1:T(4,128)S(1)}, f32[8,3]{0,1:T(4,128)}, u32[]{:S(2)}) copy-start(f32[8,3]{0,1:T(4,128)} %param.12) | copy-start | bytes 292
  2.6 11.5 %copy-start.7 = (s32[8,8]{1,0:T(8,128)S(1)}, s32[8,8]{1,0:T(8,128)}, u32[]{:S(2)}) copy-start(s32[8,8]{1,0:T(8,128)} %param.13) | copy-start | bytes 772
  2.6 37.1 %all-to-all-start = ((f32[128,25,1,128]{3,2,1,0:T(1,128)}), f32[128,25,1,128]{3,2,1,0:T(1,128)S(1)}, u32[]{:S(2)}, u32[]{:S(2)}) async-start(f32[128,25,1,128]{3,2,1,0:T(1,128)} %bitcast.23), calls=%async_computation | async-start | bytes 3276800 | tf_op jit(solution)/shard_map/all_to_all | solution.py:221
  16.5 3.8 %copy-start.6 = (f32[3,100,8]{1,2,0:T(8,128)S(1)}, f32[3,100,8]{1,2,0:T(8,128)}, u32[]{:S(2)}) copy-start(f32[3,100,8]{1,2,0:T(8,128)} %param.9) | copy-start | bytes 28804
  16.5 4.2 %copy-start.2 = (f32[3]{0:T(128)S(1)}, f32[3]{0:T(128)}, u32[]{:S(2)}) copy-start(f32[3]{0:T(128)} %occ_ref.1) | copy-start | bytes 40
  16.5 4.2 %copy-start.3 = (s32[3]{0:T(128)S(1)}, s32[3]{0:T(128)}, u32[]{:S(2)}) copy-start(s32[3]{0:T(128)} %shift_ref.1) | copy-start | bytes 40
  16.5 4.2 %copy-start.4 = (f32[128,256]{1,0:T(8,128)S(1)}, f32[128,256]{1,0:T(8,128)}, u32[]{:S(2)}) copy-start(f32[128,256]{1,0:T(8,128)} %constant.10.clone.cols_ref) | copy-start | bytes 393220
  20.7 0.9 %copy-start.1 = (f32[3,128,128]{2,1,0:T(8,128)S(1)}, f32[3,128,128]{2,1,0:T(8,128)}, u32[]{:S(2)}) copy-start(f32[3,128,128]{2,1,0:T(8,128)} %tile.10.mix_ref) | copy-start | bytes 589828
  21.6 0.9 %copy-start.5 = (f32[256,16]{1,0:T(8,128)S(1)}, f32[256,16]{1,0:T(8,128)}, u32[]{:S(2)}) copy-start(f32[256,16]{1,0:T(8,128)} %constant.11.clone.rows_ref) | copy-start | bytes 49156

commit v3 on v2

--- a/solution.py
+++ b/solution.py
@@ -1,3 +1,5 @@
+import functools
+
 import jax
 import jax.numpy as jnp
 import numpy as np
@@ -34,18 +36,18 @@
     return pltpu.roll(value, lanes % LANES, 1) if lanes % LANES else value
 
 
-def pack_kernel(green_ref, out_ref, held_ref, message_ref, rest_ref, sems, out_sems):
+def pack_kernel(spots, green_ref, out_ref, held_ref, message_ref, rest_ref, sems, out_sems):
     rest_copy = pltpu.make_async_copy(
         green_ref.at[pl.ds(384, 16), :], held_ref.at[pl.ds(384, 16), :], sems.at[2]
     )
     rest_copy.start()
     copies = []
-    for half in range(2):
-        place = (pl.ds(0, 384), pl.ds(512 * half, 512))
+    for part in range(2):
+        place = (pl.ds(0, 384), pl.ds(512 * part, 512))
         copies.append(
-            pltpu.make_async_copy(green_ref.at[place], held_ref.at[place], sems.at[half])
-        )
-        copies[half].start()
+            pltpu.make_async_copy(green_ref.at[place], held_ref.at[place], sems.at[part])
+        )
+        copies[part].start()
     rest_copy.wait()
     rest_ref[...] = jnp.concatenate(
         [held_ref[384:400, LANES * g : LANES * (g + 1)] for g in range(8)], axis=0
@@ -57,29 +59,44 @@
         for atom in range(8):
             piece = turn(pieces[atom], 16 * (atom - group))
             joined = piece if joined is None else jnp.where(lane < 16 * atom, joined, piece)
-        message_ref[pl.ds(400 * group + 24, 16, stride=ROWS), :] = joined
-    for group in range(8):
-        if group % 4 == 0:
+        for first in range(0, 16, 4):
+            row = ROWS * spots[16 * group + first] + 24
+            message_ref[pl.ds(row, 4, stride=ROWS), :] = joined[first : first + 4, :]
+    waited, filled, sent = set(), [0] * 8, []
+    for group in (0, 2, 4, 6, 1, 3, 5, 7):
+        if group // 4 not in waited:
             copies[group // 4].wait()
+            waited.add(group // 4)
         for tile in range(3):
             turned = held_ref[
                 LANES * tile : LANES * (tile + 1), LANES * group : LANES * (group + 1)
             ].T
             for owner in range(16):
-                row = 400 * group + ROWS * owner + 8 * tile
+                row = ROWS * spots[16 * group + owner] + 8 * tile
                 message_ref[row : row + 8, :] = turned[8 * owner : 8 * owner + 8, :]
-        place = pl.ds(400 * group, 400)
-        copies.append(
-            pltpu.make_async_copy(message_ref.at[place], out_ref.at[place], out_sems.at[group])
-        )
-        copies[-1].start()
-    for copy in copies[2:]:
+        for owner in range(16):
+            block = spots[16 * group + owner] // 16
+            filled[block] += 1
+            if filled[block] == 16:
+                place = pl.ds(400 * block, 400)
+                sent.append(
+                    pltpu.make_async_copy(
+                        message_ref.at[place], out_ref.at[place], out_sems.at[block]
+                    )
+                )
+                sent[-1].start()
+    for copy in sent:
         copy.wait()
 
 
-def unpack_kernel(in_ref, out_ref, held_ref, rest_ref, sems):
+def unpack_kernel(spots, in_ref, out_ref, held_ref, rest_ref, sems):
     lane = lax.broadcasted_iota(jnp.int32, (16, LANES), 1)
-    pieces = [in_ref[pl.ds(400 * group + 24, 16, stride=ROWS), :] for group in range(8)]
+    pieces = []
+    for group in range(8):
+        rows = [ROWS * spots[16 * group + first] + 24 for first in range(0, 16, 4)]
+        pieces.append(
+            jnp.concatenate([in_ref[pl.ds(row, 4, stride=ROWS), :] for row in rows], axis=0)
+        )
     for atom in range(8):
         joined = None
         for group in range(8):
@@ -99,7 +116,7 @@
     copies[0].start()
     for group in range(8):
         for tile in range(3):
-            rows = [400 * group + ROWS * owner + 8 * tile for owner in range(16)]
+            rows = [ROWS * spots[16 * group + owner] + 8 * tile for owner in range(16)]
             held_ref[
                 LANES * tile : LANES * (tile + 1), LANES * group : LANES * (group + 1)
             ] = jnp.concatenate([in_ref[row : row + 8, :] for row in rows], axis=0).T
@@ -113,7 +130,19 @@
 
 
 def prepare_kernel(
-    occ_ref, shift_ref, couple_ref, mix_ref, cols_ref, rows_ref, out_ref, high_ref, low_ref
+    occ_ref,
+    shift_ref,
+    couple_ref,
+    mix_ref,
+    cols_ref,
+    rows_ref,
+    pick_ref,
+    picked_ref,
+    row_ref,
+    col_ref,
+    out_ref,
+    high_ref,
+    low_ref,
 ):
     spread = lax.dot(
         couple_ref[...], cols_ref[...], precision=HIGHEST, preferred_element_type=jnp.float32
@@ -131,13 +160,19 @@
         high, low = split(first * second)
         out_ref[index, :, :LANES] = high[:DEPTH]
         out_ref[index, :, LANES:] = low[:DEPTH]
-    row = lax.broadcasted_iota(jnp.int32, (POINTS, POINTS), 0) >> 3
-    col = lax.broadcasted_iota(jnp.int32, (POINTS, POINTS), 1) >> 3
+    row = jnp.broadcast_to(row_ref[...], (POINTS, POINTS))
+    col = jnp.broadcast_to(col_ref[...], (POINTS, POINTS))
     for mode in range(MODES):
         step = shift_ref[mode]
         above = col == row + step
         below = col == row - step
-        mixing = mix_ref[mode]
+        mixing = lax.dot(
+            lax.dot(
+                pick_ref[:, :8], mix_ref[mode], precision=HIGHEST,
+                preferred_element_type=jnp.float32,
+            ),
+            picked_ref[...], precision=HIGHEST, preferred_element_type=jnp.float32,
+        )
         for kind in range(2):
             upper = occ_ref[mode] + (1.0 - kind)
             lower = occ_ref[mode] + float(kind)
@@ -217,9 +252,14 @@
     return jnp.asarray(cols), jnp.asarray(rows)
 
 
-def exchange(message):
+def exchange(message, order):
     moved = lax.all_to_all(
-        message.reshape(POINTS, ROWS, 1, LANES), AXES, split_axis=0, concat_axis=0, tiled=True
+        message.reshape(POINTS, ROWS, 1, LANES),
+        AXES,
+        split_axis=0,
+        concat_axis=0,
+        tiled=True,
+        axis_index_groups=[order],
     )
     return moved.reshape(POINTS * ROWS, LANES)
 
@@ -231,14 +271,17 @@
     return jnp.einsum("kjq,qm->mkj", onehot, branch_weight, precision=HIGHEST)
 
 
-def on_device(green_blocks, couple_matrix, occupation, energy_shift, branch_weight, pair_branch):
+def on_device(
+    order, green_blocks, couple_matrix, occupation, energy_shift, branch_weight, pair_branch
+):
     f32, bf16 = jnp.float32, jnp.bfloat16
+    spots = [order.index(device) for device in range(POINTS)]
     smem = pl.BlockSpec(memory_space=pltpu.SMEM)
     vmem = pl.BlockSpec(memory_space=pltpu.VMEM)
     hbm = pl.BlockSpec(memory_space=pltpu.HBM)
     tiles = green_blocks.shape[4] // LANES
     message = pl.pallas_call(
-        pack_kernel,
+        functools.partial(pack_kernel, spots),
         in_specs=[hbm],
         out_specs=hbm,
         out_shape=pltpu.HBM((POINTS * ROWS, LANES), f32),
@@ -252,15 +295,19 @@
         compiler_params=PARAMS,
         name="pack",
     )(constrain(green_blocks.reshape(400, tiles * LANES), pltpu.HBM))
-    received = exchange(message)
-
-    table = jnp.tile(mixing(branch_weight, pair_branch) / pair_branch.shape[0], (1, 16, 16))
+    received = exchange(message, order)
+
+    moments = pair_branch.shape[0]
+    energies = jnp.asarray([place // moments for place in order], jnp.int32)
+    pick = np.zeros((POINTS, moments), np.float32)
+    pick[np.arange(POINTS), [place % moments for place in order]] = 1.0
+    table = mixing(branch_weight, pair_branch) / moments
     turned = couple_matrix.reshape(MODES, ORB, ORB, ATOMS_HERE).transpose(3, 0, 2, 1)
     turned = jnp.pad(turned, ((0, 0), (0, 0), (0, 6), (0, LANES - ORB))).reshape(-1, LANES)
     cols, rows = constants()
     weight, high, low = pl.pallas_call(
         prepare_kernel,
-        in_specs=[smem, smem, vmem, vmem, vmem, vmem],
+        in_specs=[smem, smem] + [vmem] * 8,
         out_specs=[vmem, vmem, vmem],
         out_shape=[
             pltpu.VMEM((ATOMS_HERE * MODES, DEPTH, 2 * LANES), bf16),
@@ -270,7 +317,18 @@
         compiler_params=PARAMS,
         cost_estimate=pl.CostEstimate(flops=10**9, bytes_accessed=4 * 10**6, transcendentals=0),
         name="prepare",
-    )(occupation, energy_shift, turned, table, cols, rows)
+    )(
+        occupation,
+        energy_shift,
+        turned,
+        jnp.pad(table, ((0, 0), (0, 0), (0, LANES - moments))),
+        cols,
+        rows,
+        jnp.asarray(np.pad(pick, ((0, 0), (0, LANES - moments)))),
+        jnp.asarray(np.pad(pick.T, ((0, LANES - moments), (0, 0)))),
+        energies[:, None],
+        energies[None, :],
+    )
 
     result = pl.pallas_call(
         compute_kernel,
@@ -280,9 +338,9 @@
         compiler_params=PARAMS,
         name="compute",
     )(*(constrain(value, pltpu.VMEM) for value in (received, weight, high, low)))
-    returned = exchange(result)
+    returned = exchange(result, order)
     out = pl.pallas_call(
-        unpack_kernel,
+        functools.partial(unpack_kernel, spots),
         in_specs=[vmem],
         out_specs=hbm,
         out_shape=pltpu.HBM((400, tiles * LANES), f32),
@@ -297,6 +355,15 @@
     return out.reshape(green_blocks.shape)
 
 
+def places(mesh):
+    def key(place):
+        energy, momentum = divmod(place, 8)
+        z = 2 * (momentum // 4) + (energy // 2) % 2
+        return energy % 2, z, energy // 4, momentum % 4
+
+    return sorted(range(mesh.size), key=key)
+
+
 def solution(mesh):
     in_specs = (
         P(None, "energy", "momentum", None, None),
@@ -307,6 +374,7 @@
         P(),
     )
     out_specs = P(None, "energy", "momentum", None, None)
+    order = places(mesh)
     return jax.shard_map(
-        on_device, mesh=mesh, in_specs=in_specs, out_specs=out_specs, check_vma=False
-    )
+        functools.partial(on_device, order), mesh=mesh, in_specs=in_specs, out_specs=out_specs, check_vma=False
+    )

time: 74.9 us -> 73.5 us (0.981)
  local copies, waits for them, and re-layouts: 7.99 us -> 3.84 us
  waiting for transfers between devices: 12.9 us -> 15 us
    another operation x2 -> x0, local copies, waits for them, and re-layouts: 5.76 us -> none  [on_device(): jnp.tile(mixing(branch_weight, pair_branch) / pair_branch.shape[0], (1, 1...]
    all_to_all x1, waiting for transfers between devices: 12.9 us -> 15 us  [exchange(): lax.all_to_all(message.reshape(POINTS, ROWS, 1, LANES), AXES, split_axis=...]
    unnamed x17 -> x23, local copies, waits for them, and re-layouts: 2.11 us -> 3.72 us
  transfers between devices with their start and end apart: 1 -> 1, of which waited for: 1 -> 1; matrix products, arithmetic and copies ran while one was open for 9% -> 1% of each run, Pallas kernels for 6% -> 6%
where the time goes in v3:
time: 73.5 us; the launch traced here: 73.1 us
  blocking collectives  29.5 us (40%)
  waiting for transfers between devices  15 us (20%)
  Pallas kernels  12.7 us (17%)
  starting transfers between devices  11.5 us (16%)
  local copies, waits for them, and re-layouts  3.84 us (5%)
    all_to_all x1, blocking collectives, exchange(): lax.all_to_all(message.reshape(POINTS, ROWS, 1, LANES), AXES, split_axis=...  29.5 us
    all_to_all x1, waiting for transfers between devices, exchange(): lax.all_to_all(message.reshape(POINTS, ROWS, 1, LANES), AXES, split_axis=...  15 us
    all_to_all x1, starting transfers between devices, exchange(): lax.all_to_all(message.reshape(POINTS, ROWS, 1, LANES), AXES, split_axis=...  11.5 us
    pallas_call x1, Pallas kernels, on_device(): pl.pallas_call(prepare_kernel, in_specs=[smem, smem] + [vmem] * 8, out_sp...  4.64 us
    unnamed x23, local copies, waits for them, and re-layouts  3.72 us
    pallas_call x1, Pallas kernels, on_device(): pl.pallas_call(compute_kernel, in_specs=[vmem] * 4, out_specs=vmem, out_s...  3.67 us
    pallas_call x1, Pallas kernels, on_device(): pl.pallas_call(functools.partial(pack_kernel, spots), in_specs=[hbm], out...  2.84 us
    pallas_call x1, Pallas kernels, on_device(): pl.pallas_call(functools.partial(unpack_kernel, spots), in_specs=[vmem],...  1.55 us
  transfers between devices with their start and end apart: 1, of which 1 were waited for; matrix products, arithmetic and copies ran while one was open for 1% of the time, Pallas kernels for 6%

profile of v3, /device:TPU:1, one launch (start us, length us, event | category | flops | bytes accessed | tf_op | source)
XLA Modules:
  0.0 73.1 jit_solution(3114479519307100871)
XLA Ops:
  0.0 0.0 copy-start
  0.0 2.8 %pack.1 = f32[3200,128]{1,0:T(8,128)} custom-call(f32[400,1024]{1,0:T(8,128)} %bitcast.22), custom_call_target="tpu_custom_call" | custom-call | tf_op jit(solution)/shard_map/pack/pallas_call | solution.py:283
  2.8 0.0 copy-start.9
  2.9 0.0 copy-start.10
  2.9 0.0 copy-start.1
  2.9 0.0 copy-start.2
  2.9 0.0 copy-start.3
  2.9 0.0 copy-start.8
  2.9 11.5 %all-to-all-start = ((f32[128,25,1,128]{3,2,1,0:T(1,128)}), f32[128,25,1,128]{3,2,1,0:T(1,128)S(1)}, u32[]{:S(2)}, u32[]{:S(2)}) async-start(f32[128,25,1,128]{3,2,1,0:T(1,128)} %bitcast.21), calls=%async_computation | async-start | bytes 3276800 | tf_op jit(solution)/shard_map/all_to_all | solution.py:256
  14.4 0.0 copy-done.9
  14.4 0.1 reshape.28
  14.6 0.3 copy.23
  14.8 0.0 copy-done
  14.9 0.4 fusion
  15.3 0.0 copy-start.4
  15.3 0.9 %copy-done.4 = f32[256,16]{1,0:T(8,128)S(1)} copy-done((f32[256,16]{1,0:T(8,128)S(1)}, f32[256,16]{1,0:T(8,128)}, u32[]{:S(2)}) %copy-start.4) | copy-done | bytes 16408
  16.2 0.8 %copy-done.5 = f32[128,128]{1,0:T(8,128)S(1)} copy-done((f32[128,128]{1,0:T(8,128)S(1)}, f32[128,128]{1,0:T(8,128)}, u32[]{:S(2)}) %copy-start.5) | copy-done | bytes 65560
  17.1 0.8 %copy-done.6 = f32[128,128]{1,0:T(8,128)S(1)} copy-done((f32[128,128]{1,0:T(8,128)S(1)}, f32[128,128]{1,0:T(8,128)}, u32[]{:S(2)}) %copy-start.6) | copy-done | bytes 65560
  17.9 0.8 %copy-done.7 = s32[128,1]{1,0:T(8,128)S(1)} copy-done((s32[128,1]{1,0:T(8,128)S(1)}, s32[128,1]{1,0:T(8,128)}, u32[]{:S(2)}) %copy-start.7) | copy-done | bytes 536
  18.7 4.6 %prepare.1 = (bf16[24,112,256]{2,1,0:T(8,128)(2,1)S(1)}, bf16[2,384,128]{2,1,0:T(8,128)(2,1)S(1)}, bf16[2,384,128]{2,1,0:T(8,128)(2,1)S(1)}) custom-call(f32[3]{0:T(128)S(1)} %copy-done.1, s32[3]{0:T(128)S(1)} %copy-done.2, f32[384,128]{1,0:T(8,128)S(1)} %bitcast.20, f32[3,8,128]{2,1,0:T(8,128)S(1)} %pad.9.mix_ref, f32[128,256]{1,0:T(8,128)S(1)} %copy-done.3, ...), custom_call_target="tpu_custom_call" | custom-call | flops 1000000000 | bytes 4000000 | tf_op jit(solution)/shard_map/prepare/pallas_call | solution.py:308
  23.4 15.0 %all-to-all-done = f32[128,25,1,128]{3,2,1,0:T(1,128)S(1)} async-done(((f32[128,25,1,128]{3,2,1,0:T(1,128)}), f32[128,25,1,128]{3,2,1,0:T(1,128)S(1)}, u32[]{:S(2)}, u32[]{:S(2)}) %all-to-all-start) | async-done | bytes 1638432 | tf_op jit(solution)/shard_map/all_to_all | solution.py:256
  38.4 3.7 %compute.1 = f32[3200,128]{1,0:T(8,128)S(1)} custom-call(f32[3200,128]{1,0:T(8,128)S(1)} %bitcast.17, bf16[24,112,256]{2,1,0:T(8,128)(2,1)S(1)} %get-tuple-element.8.weight_ref, bf16[2,384,128]{2,1,0:T(8,128)(2,1)S(1)} %get-tuple-element.9.high_ref, bf16[2,384,128]{2,1,0:T(8,128)(2,1)S(1)} %get-tuple-element.10.low_ref), custom_call_target="tpu_custom_call" | custom-call | tf_op jit(solution)/shard_map/compute/pallas_call | solution.py:333
  42.1 29.5 %all_to_all.10 = f32[128,25,1,128]{3,2,1,0:T(1,128)S(1)} all-to-all(f32[128,25,1,128]{3,2,1,0:T(1,128)S(1)} %bitcast.18), channel_id=1, replica_groups={{0,1,2,3,32,33,34,35,64,65,66,67,96,97,98,99,16,17,18,19,48,49,50,51,80..., dimensions={0} | all-to-all | bytes 3276800 | tf_op jit(solution)/shard_map/all_to_all | solution.py:256
  71.6 1.5 %unpack.1 = f32[400,1024]{1,0:T(8,128)} custom-call(f32[3200,128]{1,0:T(8,128)S(1)} %bitcast.19), custom_call_target="tpu_custom_call" | custom-call | tf_op jit(solution)/shard_map/unpack/pallas_call | solution.py:342
  (11 shorter events, 0.0 us)
Async XLA Ops:
  0.0 14.8 %copy-start = (f32[8,3]{0,1:T(4,128)S(1)}, f32[8,3]{0,1:T(4,128)}, u32[]{:S(2)}) copy-start(f32[8,3]{0,1:T(4,128)} %param.15) | copy-start | bytes 292
  2.8 11.6 %copy-start.9 = (f32[3,100,8]{1,2,0:T(8,128)S(1)}, f32[3,100,8]{1,2,0:T(8,128)}, u32[]{:S(2)}) copy-start(f32[3,100,8]{1,2,0:T(8,128)} %param.12) | copy-start | bytes 28804
  2.9 12.0 %copy-start.10 = (s32[8,8]{1,0:T(8,128)S(1)}, s32[8,8]{1,0:T(8,128)}, u32[]{:S(2)}) copy-start(s32[8,8]{1,0:T(8,128)} %param.16) | copy-start | bytes 772
  2.9 12.4 %copy-start.1 = (f32[3]{0:T(128)S(1)}, f32[3]{0:T(128)}, u32[]{:S(2)}) copy-start(f32[3]{0:T(128)} %occ_ref.1) | copy-start | bytes 40
  2.9 12.4 %copy-start.2 = (s32[3]{0:T(128)S(1)}, s32[3]{0:T(128)}, u32[]{:S(2)}) copy-start(s32[3]{0:T(128)} %shift_ref.1) | copy-start | bytes 40
  2.9 12.4 %copy-start.3 = (f32[128,256]{1,0:T(8,128)S(1)}, f32[128,256]{1,0:T(8,128)}, u32[]{:S(2)}) copy-start(f32[128,256]{1,0:T(8,128)} %constant.17.clone.cols_ref) | copy-start | bytes 393220
  2.9 12.4 %copy-start.8 = (s32[1,128]{1,0:T(1,128)S(1)}, s32[1,128]{1,0:T(1,128)}, u32[]{:S(2)}) copy-start(s32[1,128]{1,0:T(1,128)} %constant.28.col_ref) | copy-start | bytes 1540
  2.9 35.5 %all-to-all-start = ((f32[128,25,1,128]{3,2,1,0:T(1,128)}), f32[128,25,1,128]{3,2,1,0:T(1,128)S(1)}, u32[]{:S(2)}, u32[]{:S(2)}) async-start(f32[128,25,1,128]{3,2,1,0:T(1,128)} %bitcast.21), calls=%async_computation | async-start | bytes 3276800 | tf_op jit(solution)/shard_map/all_to_all | solution.py:256
  15.3 0.9 %copy-start.4 = (f32[256,16]{1,0:T(8,128)S(1)}, f32[256,16]{1,0:T(8,128)}, u32[]{:S(2)}) copy-start(f32[256,16]{1,0:T(8,128)} %constant.18.clone.rows_ref) | copy-start | bytes 49156
  16.2 0.8 %copy-start.5 = (f32[128,128]{1,0:T(8,128)S(1)}, f32[128,128]{1,0:T(8,128)}, u32[]{:S(2)}) copy-start(f32[128,128]{1,0:T(8,128)} %constant.19.clone.pick_ref) | copy-start | bytes 196612
  17.1 0.8 %copy-start.6 = (f32[128,128]{1,0:T(8,128)S(1)}, f32[128,128]{1,0:T(8,128)}, u32[]{:S(2)}) copy-start(f32[128,128]{1,0:T(8,128)} %constant.20.clone.picked_ref) | copy-start | bytes 196612
  17.9 0.8 %copy-start.7 = (s32[128,1]{1,0:T(8,128)S(1)}, s32[128,1]{1,0:T(8,128)}, u32[]{:S(2)}) copy-start(s32[128,1]{1,0:T(8,128)} %constant.27.row_ref) | copy-start | bytes 1540

commit v4 on v3

--- a/solution.py
+++ b/solution.py
@@ -94,8 +94,9 @@
     pieces = []
     for group in range(8):
         rows = [ROWS * spots[16 * group + first] + 24 for first in range(0, 16, 4)]
+        step = ROWS * (spots[1] - spots[0])
         pieces.append(
-            jnp.concatenate([in_ref[pl.ds(row, 4, stride=ROWS), :] for row in rows], axis=0)
+            jnp.concatenate([in_ref[pl.ds(row, 4, stride=step), :] for row in rows], axis=0)
         )
     for atom in range(8):
         joined = None
@@ -272,16 +273,17 @@
 
 
 def on_device(
-    order, green_blocks, couple_matrix, occupation, energy_shift, branch_weight, pair_branch
+    out_order, back_order, green_blocks, couple_matrix, occupation, energy_shift, branch_weight, pair_branch
 ):
     f32, bf16 = jnp.float32, jnp.bfloat16
-    spots = [order.index(device) for device in range(POINTS)]
+    out_spots = [out_order.index(device) for device in range(POINTS)]
+    back_spots = [back_order.index(device) for device in range(POINTS)]
     smem = pl.BlockSpec(memory_space=pltpu.SMEM)
     vmem = pl.BlockSpec(memory_space=pltpu.VMEM)
     hbm = pl.BlockSpec(memory_space=pltpu.HBM)
     tiles = green_blocks.shape[4] // LANES
     message = pl.pallas_call(
-        functools.partial(pack_kernel, spots),
+        functools.partial(pack_kernel, out_spots),
         in_specs=[hbm],
         out_specs=hbm,
         out_shape=pltpu.HBM((POINTS * ROWS, LANES), f32),
@@ -295,12 +297,15 @@
         compiler_params=PARAMS,
         name="pack",
     )(constrain(green_blocks.reshape(400, tiles * LANES), pltpu.HBM))
-    received = exchange(message, order)
+    received = exchange(message, out_order)
 
     moments = pair_branch.shape[0]
-    energies = jnp.asarray([place // moments for place in order], jnp.int32)
-    pick = np.zeros((POINTS, moments), np.float32)
-    pick[np.arange(POINTS), [place % moments for place in order]] = 1.0
+    picks, energies = [], []
+    for order in (back_order, out_order):
+        pick = np.zeros((POINTS, moments), np.float32)
+        pick[np.arange(POINTS), [place % moments for place in order]] = 1.0
+        picks.append(pick)
+        energies.append(jnp.asarray([place // moments for place in order], jnp.int32))
     table = mixing(branch_weight, pair_branch) / moments
     turned = couple_matrix.reshape(MODES, ORB, ORB, ATOMS_HERE).transpose(3, 0, 2, 1)
     turned = jnp.pad(turned, ((0, 0), (0, 0), (0, 6), (0, LANES - ORB))).reshape(-1, LANES)
@@ -324,10 +329,10 @@
         jnp.pad(table, ((0, 0), (0, 0), (0, LANES - moments))),
         cols,
         rows,
-        jnp.asarray(np.pad(pick, ((0, 0), (0, LANES - moments)))),
-        jnp.asarray(np.pad(pick.T, ((0, LANES - moments), (0, 0)))),
-        energies[:, None],
-        energies[None, :],
+        jnp.asarray(np.pad(picks[0], ((0, 0), (0, LANES - moments)))),
+        jnp.asarray(np.pad(picks[1].T, ((0, LANES - moments), (0, 0)))),
+        energies[0][:, None],
+        energies[1][None, :],
     )
 
     result = pl.pallas_call(
@@ -338,9 +343,9 @@
         compiler_params=PARAMS,
         name="compute",
     )(*(constrain(value, pltpu.VMEM) for value in (received, weight, high, low)))
-    returned = exchange(result, order)
+    returned = exchange(result, back_order)
     out = pl.pallas_call(
-        functools.partial(unpack_kernel, spots),
+        functools.partial(unpack_kernel, back_spots),
         in_specs=[vmem],
         out_specs=hbm,
         out_shape=pltpu.HBM((400, tiles * LANES), f32),
@@ -355,11 +360,11 @@
     return out.reshape(green_blocks.shape)
 
 
-def places(mesh):
+def places(mesh, z_first):
     def key(place):
         energy, momentum = divmod(place, 8)
-        z = 2 * (momentum // 4) + (energy // 2) % 2
-        return energy % 2, z, energy // 4, momentum % 4
+        chip = (2 * (momentum // 4) + (energy // 2) % 2, energy // 4, momentum % 4)
+        return (energy % 2,) + (chip if z_first else chip[::-1])
 
     return sorted(range(mesh.size), key=key)
 
@@ -374,7 +379,7 @@
         P(),
     )
     out_specs = P(None, "energy", "momentum", None, None)
-    order = places(mesh)
+    orders = places(mesh, True), places(mesh, False)
     return jax.shard_map(
-        functools.partial(on_device, order), mesh=mesh, in_specs=in_specs, out_specs=out_specs, check_vma=False
-    )
+        functools.partial(on_device, *orders), mesh=mesh, in_specs=in_specs, out_specs=out_specs, check_vma=False
+    )

time: 73.5 us -> 73.1 us (level)
  no operation moved by 1% of the time
where the time goes in v4:
time: 73.1 us; the launch traced here: 72.7 us
  blocking collectives  29 us (40%)
  waiting for transfers between devices  15 us (21%)
  Pallas kernels  12.7 us (17%)
  starting transfers between devices  11.5 us (16%)
  local copies, waits for them, and re-layouts  3.84 us (5%)
    all_to_all x1, blocking collectives, exchange(): lax.all_to_all(message.reshape(POINTS, ROWS, 1, LANES), AXES, split_axis=...  29 us
    all_to_all x1, waiting for transfers between devices, exchange(): lax.all_to_all(message.reshape(POINTS, ROWS, 1, LANES), AXES, split_axis=...  15 us
    all_to_all x1, starting transfers between devices, exchange(): lax.all_to_all(message.reshape(POINTS, ROWS, 1, LANES), AXES, split_axis=...  11.5 us
    pallas_call x1, Pallas kernels, on_device(): pl.pallas_call(prepare_kernel, in_specs=[smem, smem] + [vmem] * 8, out_sp...  4.64 us
    unnamed x23, local copies, waits for them, and re-layouts  3.72 us
    pallas_call x1, Pallas kernels, on_device(): pl.pallas_call(compute_kernel, in_specs=[vmem] * 4, out_specs=vmem, out_s...  3.67 us
    pallas_call x1, Pallas kernels, on_device(): pl.pallas_call(functools.partial(pack_kernel, out_spots), in_specs=[hbm],...  2.84 us
    pallas_call x1, Pallas kernels, on_device(): pl.pallas_call(functools.partial(unpack_kernel, back_spots), in_specs=[vm...  1.55 us
  transfers between devices with their start and end apart: 1, of which 1 were waited for; matrix products, arithmetic and copies ran while one was open for 1% of the time, Pallas kernels for 6%

profile of v4, /device:TPU:1, one launch (start us, length us, event | category | flops | bytes accessed | tf_op | source)
XLA Modules:
  0.0 72.7 jit_solution(12850045232703109980)
XLA Ops:
  0.0 0.0 copy-start
  0.0 2.8 %pack.1 = f32[3200,128]{1,0:T(8,128)} custom-call(f32[400,1024]{1,0:T(8,128)} %bitcast.22), custom_call_target="tpu_custom_call" | custom-call | tf_op jit(solution)/shard_map/pack/pallas_call | solution.py:285
  2.8 0.0 copy-start.9
  2.9 0.0 copy-start.10
  2.9 0.0 copy-start.1
  2.9 0.0 copy-start.2
  2.9 0.0 copy-start.3
  2.9 0.0 copy-start.8
  2.9 11.5 %all-to-all-start = ((f32[128,25,1,128]{3,2,1,0:T(1,128)}), f32[128,25,1,128]{3,2,1,0:T(1,128)S(1)}, u32[]{:S(2)}, u32[]{:S(2)}) async-start(f32[128,25,1,128]{3,2,1,0:T(1,128)} %bitcast.21), calls=%async_computation | async-start | bytes 3276800 | tf_op jit(solution)/shard_map/all_to_all | solution.py:257
  14.4 0.0 copy-done.9
  14.4 0.1 reshape.28
  14.6 0.3 copy.24
  14.8 0.0 copy-done
  14.9 0.4 fusion
  15.3 0.0 copy-start.4
  15.3 0.9 %copy-done.4 = f32[256,16]{1,0:T(8,128)S(1)} copy-done((f32[256,16]{1,0:T(8,128)S(1)}, f32[256,16]{1,0:T(8,128)}, u32[]{:S(2)}) %copy-start.4) | copy-done | bytes 16408
  16.2 0.8 %copy-done.5 = f32[128,128]{1,0:T(8,128)S(1)} copy-done((f32[128,128]{1,0:T(8,128)S(1)}, f32[128,128]{1,0:T(8,128)}, u32[]{:S(2)}) %copy-start.5) | copy-done | bytes 65560
  17.1 0.8 %copy-done.6 = f32[128,128]{1,0:T(8,128)S(1)} copy-done((f32[128,128]{1,0:T(8,128)S(1)}, f32[128,128]{1,0:T(8,128)}, u32[]{:S(2)}) %copy-start.6) | copy-done | bytes 65560
  17.9 0.8 %copy-done.7 = s32[128,1]{1,0:T(8,128)S(1)} copy-done((s32[128,1]{1,0:T(8,128)S(1)}, s32[128,1]{1,0:T(8,128)}, u32[]{:S(2)}) %copy-start.7) | copy-done | bytes 536
  18.7 4.6 %prepare.1 = (bf16[24,112,256]{2,1,0:T(8,128)(2,1)S(1)}, bf16[2,384,128]{2,1,0:T(8,128)(2,1)S(1)}, bf16[2,384,128]{2,1,0:T(8,128)(2,1)S(1)}) custom-call(f32[3]{0:T(128)S(1)} %copy-done.1, s32[3]{0:T(128)S(1)} %copy-done.2, f32[384,128]{1,0:T(8,128)S(1)} %bitcast.20, f32[3,8,128]{2,1,0:T(8,128)S(1)} %pad.9.mix_ref, f32[128,256]{1,0:T(8,128)S(1)} %copy-done.3, ...), custom_call_target="tpu_custom_call" | custom-call | flops 1000000000 | bytes 4000000 | tf_op jit(solution)/shard_map/prepare/pallas_call | solution.py:313
  23.4 15.0 %all-to-all-done = f32[128,25,1,128]{3,2,1,0:T(1,128)S(1)} async-done(((f32[128,25,1,128]{3,2,1,0:T(1,128)}), f32[128,25,1,128]{3,2,1,0:T(1,128)S(1)}, u32[]{:S(2)}, u32[]{:S(2)}) %all-to-all-start) | async-done | bytes 1638432 | tf_op jit(solution)/shard_map/all_to_all | solution.py:257
  38.4 3.7 %compute.1 = f32[3200,128]{1,0:T(8,128)S(1)} custom-call(f32[3200,128]{1,0:T(8,128)S(1)} %bitcast.17, bf16[24,112,256]{2,1,0:T(8,128)(2,1)S(1)} %get-tuple-element.8.weight_ref, bf16[2,384,128]{2,1,0:T(8,128)(2,1)S(1)} %get-tuple-element.9.high_ref, bf16[2,384,128]{2,1,0:T(8,128)(2,1)S(1)} %get-tuple-element.10.low_ref), custom_call_target="tpu_custom_call" | custom-call | tf_op jit(solution)/shard_map/compute/pallas_call | solution.py:338
  42.1 29.0 %all_to_all.10 = f32[128,25,1,128]{3,2,1,0:T(1,128)S(1)} all-to-all(f32[128,25,1,128]{3,2,1,0:T(1,128)S(1)} %bitcast.18), channel_id=1, replica_groups={{0,16,4,20,32,48,36,52,64,80,68,84,96,112,100,116,1,17,5,21,33,49,37,53..., dimensions={0} | all-to-all | bytes 3276800 | tf_op jit(solution)/shard_map/all_to_all | solution.py:257
  71.1 1.6 %unpack.1 = f32[400,1024]{1,0:T(8,128)} custom-call(f32[3200,128]{1,0:T(8,128)S(1)} %bitcast.19), custom_call_target="tpu_custom_call" | custom-call | tf_op jit(solution)/shard_map/unpack/pallas_call | solution.py:347
  (11 shorter events, 0.0 us)
Async XLA Ops:
  0.0 14.8 %copy-start = (f32[8,3]{0,1:T(4,128)S(1)}, f32[8,3]{0,1:T(4,128)}, u32[]{:S(2)}) copy-start(f32[8,3]{0,1:T(4,128)} %param.16) | copy-start | bytes 292
  2.8 11.6 %copy-start.9 = (f32[3,100,8]{1,2,0:T(8,128)S(1)}, f32[3,100,8]{1,2,0:T(8,128)}, u32[]{:S(2)}) copy-start(f32[3,100,8]{1,2,0:T(8,128)} %param.13) | copy-start | bytes 28804
  2.9 12.0 %copy-start.10 = (s32[8,8]{1,0:T(8,128)S(1)}, s32[8,8]{1,0:T(8,128)}, u32[]{:S(2)}) copy-start(s32[8,8]{1,0:T(8,128)} %param.17) | copy-start | bytes 772
  2.9 12.4 %copy-start.1 = (f32[3]{0:T(128)S(1)}, f32[3]{0:T(128)}, u32[]{:S(2)}) copy-start(f32[3]{0:T(128)} %occ_ref.1) | copy-start | bytes 40
  2.9 12.4 %copy-start.2 = (s32[3]{0:T(128)S(1)}, s32[3]{0:T(128)}, u32[]{:S(2)}) copy-start(s32[3]{0:T(128)} %shift_ref.1) | copy-start | bytes 40
  2.9 12.4 %copy-start.3 = (f32[128,256]{1,0:T(8,128)S(1)}, f32[128,256]{1,0:T(8,128)}, u32[]{:S(2)}) copy-start(f32[128,256]{1,0:T(8,128)} %constant.20.clone.cols_ref) | copy-start | bytes 393220
  2.9 12.4 %copy-start.8 = (s32[1,128]{1,0:T(1,128)S(1)}, s32[1,128]{1,0:T(1,128)}, u32[]{:S(2)}) copy-start(s32[1,128]{1,0:T(1,128)} %constant.31.col_ref) | copy-start | bytes 1540
  2.9 35.5 %all-to-all-start = ((f32[128,25,1,128]{3,2,1,0:T(1,128)}), f32[128,25,1,128]{3,2,1,0:T(1,128)S(1)}, u32[]{:S(2)}, u32[]{:S(2)}) async-start(f32[128,25,1,128]{3,2,1,0:T(1,128)} %bitcast.21), calls=%async_computation | async-start | bytes 3276800 | tf_op jit(solution)/shard_map/all_to_all | solution.py:257
  15.3 0.9 %copy-start.4 = (f32[256,16]{1,0:T(8,128)S(1)}, f32[256,16]{1,0:T(8,128)}, u32[]{:S(2)}) copy-start(f32[256,16]{1,0:T(8,128)} %constant.21.clone.rows_ref) | copy-start | bytes 49156
  16.2 0.8 %copy-start.5 = (f32[128,128]{1,0:T(8,128)S(1)}, f32[128,128]{1,0:T(8,128)}, u32[]{:S(2)}) copy-start(f32[128,128]{1,0:T(8,128)} %constant.22.clone.pick_ref) | copy-start | bytes 196612
  17.1 0.8 %copy-start.6 = (f32[128,128]{1,0:T(8,128)S(1)}, f32[128,128]{1,0:T(8,128)}, u32[]{:S(2)}) copy-start(f32[128,128]{1,0:T(8,128)} %constant.23.clone.picked_ref) | copy-start | bytes 196612
  17.9 0.8 %copy-start.7 = (s32[128,1]{1,0:T(8,128)S(1)}, s32[128,1]{1,0:T(8,128)}, u32[]{:S(2)}) copy-start(s32[128,1]{1,0:T(8,128)} %constant.30.row_ref) | copy-start | bytes 1540

commit v5 on v4

--- a/solution.py
+++ b/solution.py
@@ -61,7 +61,8 @@
             joined = piece if joined is None else jnp.where(lane < 16 * atom, joined, piece)
         for first in range(0, 16, 4):
             row = ROWS * spots[16 * group + first] + 24
-            message_ref[pl.ds(row, 4, stride=ROWS), :] = joined[first : first + 4, :]
+            step = ROWS * (spots[1] - spots[0])
+            message_ref[pl.ds(row, 4, stride=step), :] = joined[first : first + 4, :]
     waited, filled, sent = set(), [0] * 8, []
     for group in (0, 2, 4, 6, 1, 3, 5, 7):
         if group // 4 not in waited:
@@ -363,8 +364,8 @@
 def places(mesh, z_first):
     def key(place):
         energy, momentum = divmod(place, 8)
-        chip = (2 * (momentum // 4) + (energy // 2) % 2, energy // 4, momentum % 4)
-        return (energy % 2,) + (chip if z_first else chip[::-1])
+        x, y, z = momentum % 4, energy // 4, 2 * (momentum // 4) + (energy // 2) % 2
+        return (energy % 2,) + ((z, x, y) if z_first else (x, y, z))
 
     return sorted(range(mesh.size), key=key)
 

time: 73.1 us -> 73.1 us (level)
  no operation moved by 1% of the time
where the time goes in v5:
time: 73.1 us; the launch traced here: 72.8 us
  blocking collectives  29.7 us (41%)
  waiting for transfers between devices  14.4 us (20%)
  Pallas kernels  12.7 us (17%)
  starting transfers between devices  11.5 us (16%)
  local copies, waits for them, and re-layouts  3.84 us (5%)
    all_to_all x1, blocking collectives, exchange(): lax.all_to_all(message.reshape(POINTS, ROWS, 1, LANES), AXES, split_axis=...  29.7 us
    all_to_all x1, waiting for transfers between devices, exchange(): lax.all_to_all(message.reshape(POINTS, ROWS, 1, LANES), AXES, split_axis=...  14.4 us
    all_to_all x1, starting transfers between devices, exchange(): lax.all_to_all(message.reshape(POINTS, ROWS, 1, LANES), AXES, split_axis=...  11.5 us
    pallas_call x1, Pallas kernels, on_device(): pl.pallas_call(prepare_kernel, in_specs=[smem, smem] + [vmem] * 8, out_sp...  4.64 us
    unnamed x23, local copies, waits for them, and re-layouts  3.72 us
    pallas_call x1, Pallas kernels, on_device(): pl.pallas_call(compute_kernel, in_specs=[vmem] * 4, out_specs=vmem, out_s...  3.67 us
    pallas_call x1, Pallas kernels, on_device(): pl.pallas_call(functools.partial(pack_kernel, out_spots), in_specs=[hbm],...  2.84 us
    pallas_call x1, Pallas kernels, on_device(): pl.pallas_call(functools.partial(unpack_kernel, back_spots), in_specs=[vm...  1.55 us
  transfers between devices with their start and end apart: 1, of which 1 were waited for; matrix products, arithmetic and copies ran while one was open for 1% of the time, Pallas kernels for 6%

profile of v5, /device:TPU:1, one launch (start us, length us, event | category | flops | bytes accessed | tf_op | source)
XLA Modules:
  0.0 72.8 jit_solution(6382809087111520035)
XLA Ops:
  0.0 0.0 copy-start
  0.0 2.8 %pack.1 = f32[3200,128]{1,0:T(8,128)} custom-call(f32[400,1024]{1,0:T(8,128)} %bitcast.22), custom_call_target="tpu_custom_call" | custom-call | tf_op jit(solution)/shard_map/pack/pallas_call | solution.py:286
  2.8 0.0 copy-start.9
  2.9 0.0 copy-start.10
  2.9 0.0 copy-start.1
  2.9 0.0 copy-start.2
  2.9 0.0 copy-start.3
  2.9 0.0 copy-start.8
  2.9 11.5 %all-to-all-start = ((f32[128,25,1,128]{3,2,1,0:T(1,128)}), f32[128,25,1,128]{3,2,1,0:T(1,128)S(1)}, u32[]{:S(2)}, u32[]{:S(2)}) async-start(f32[128,25,1,128]{3,2,1,0:T(1,128)} %bitcast.21), calls=%async_computation | async-start | bytes 3276800 | tf_op jit(solution)/shard_map/all_to_all | solution.py:258
  14.4 0.0 copy-done.9
  14.4 0.1 reshape.28
  14.6 0.3 copy.24
  14.8 0.0 copy-done
  14.9 0.4 fusion
  15.3 0.0 copy-start.4
  15.3 0.9 %copy-done.4 = f32[256,16]{1,0:T(8,128)S(1)} copy-done((f32[256,16]{1,0:T(8,128)S(1)}, f32[256,16]{1,0:T(8,128)}, u32[]{:S(2)}) %copy-start.4) | copy-done | bytes 16408
  16.2 0.8 %copy-done.5 = f32[128,128]{1,0:T(8,128)S(1)} copy-done((f32[128,128]{1,0:T(8,128)S(1)}, f32[128,128]{1,0:T(8,128)}, u32[]{:S(2)}) %copy-start.5) | copy-done | bytes 65560
  17.1 0.8 %copy-done.6 = f32[128,128]{1,0:T(8,128)S(1)} copy-done((f32[128,128]{1,0:T(8,128)S(1)}, f32[128,128]{1,0:T(8,128)}, u32[]{:S(2)}) %copy-start.6) | copy-done | bytes 65560
  17.9 0.8 %copy-done.7 = s32[128,1]{1,0:T(8,128)S(1)} copy-done((s32[128,1]{1,0:T(8,128)S(1)}, s32[128,1]{1,0:T(8,128)}, u32[]{:S(2)}) %copy-start.7) | copy-done | bytes 536
  18.7 4.6 %prepare.1 = (bf16[24,112,256]{2,1,0:T(8,128)(2,1)S(1)}, bf16[2,384,128]{2,1,0:T(8,128)(2,1)S(1)}, bf16[2,384,128]{2,1,0:T(8,128)(2,1)S(1)}) custom-call(f32[3]{0:T(128)S(1)} %copy-done.1, s32[3]{0:T(128)S(1)} %copy-done.2, f32[384,128]{1,0:T(8,128)S(1)} %bitcast.20, f32[3,8,128]{2,1,0:T(8,128)S(1)} %pad.9.mix_ref, f32[128,256]{1,0:T(8,128)S(1)} %copy-done.3, ...), custom_call_target="tpu_custom_call" | custom-call | flops 1000000000 | bytes 4000000 | tf_op jit(solution)/shard_map/prepare/pallas_call | solution.py:314
  23.4 14.4 %all-to-all-done = f32[128,25,1,128]{3,2,1,0:T(1,128)S(1)} async-done(((f32[128,25,1,128]{3,2,1,0:T(1,128)}), f32[128,25,1,128]{3,2,1,0:T(1,128)S(1)}, u32[]{:S(2)}, u32[]{:S(2)}) %all-to-all-start) | async-done | bytes 1638432 | tf_op jit(solution)/shard_map/all_to_all | solution.py:258
  37.8 3.7 %compute.1 = f32[3200,128]{1,0:T(8,128)S(1)} custom-call(f32[3200,128]{1,0:T(8,128)S(1)} %bitcast.17, bf16[24,112,256]{2,1,0:T(8,128)(2,1)S(1)} %get-tuple-element.8.weight_ref, bf16[2,384,128]{2,1,0:T(8,128)(2,1)S(1)} %get-tuple-element.9.high_ref, bf16[2,384,128]{2,1,0:T(8,128)(2,1)S(1)} %get-tuple-element.10.low_ref), custom_call_target="tpu_custom_call" | custom-call | tf_op jit(solution)/shard_map/compute/pallas_call | solution.py:339
  41.5 29.7 %all_to_all.10 = f32[128,25,1,128]{3,2,1,0:T(1,128)S(1)} all-to-all(f32[128,25,1,128]{3,2,1,0:T(1,128)S(1)} %bitcast.18), channel_id=1, replica_groups={{0,16,4,20,32,48,36,52,64,80,68,84,96,112,100,116,1,17,5,21,33,49,37,53..., dimensions={0} | all-to-all | bytes 3276800 | tf_op jit(solution)/shard_map/all_to_all | solution.py:258
  71.2 1.6 %unpack.1 = f32[400,1024]{1,0:T(8,128)} custom-call(f32[3200,128]{1,0:T(8,128)S(1)} %bitcast.19), custom_call_target="tpu_custom_call" | custom-call | tf_op jit(solution)/shard_map/unpack/pallas_call | solution.py:348
  (11 shorter events, 0.0 us)
Async XLA Ops:
  0.0 14.8 %copy-start = (f32[8,3]{0,1:T(4,128)S(1)}, f32[8,3]{0,1:T(4,128)}, u32[]{:S(2)}) copy-start(f32[8,3]{0,1:T(4,128)} %param.16) | copy-start | bytes 292
  2.8 11.6 %copy-start.9 = (f32[3,100,8]{1,2,0:T(8,128)S(1)}, f32[3,100,8]{1,2,0:T(8,128)}, u32[]{:S(2)}) copy-start(f32[3,100,8]{1,2,0:T(8,128)} %param.13) | copy-start | bytes 28804
  2.9 12.0 %copy-start.10 = (s32[8,8]{1,0:T(8,128)S(1)}, s32[8,8]{1,0:T(8,128)}, u32[]{:S(2)}) copy-start(s32[8,8]{1,0:T(8,128)} %param.17) | copy-start | bytes 772
  2.9 12.4 %copy-start.1 = (f32[3]{0:T(128)S(1)}, f32[3]{0:T(128)}, u32[]{:S(2)}) copy-start(f32[3]{0:T(128)} %occ_ref.1) | copy-start | bytes 40
  2.9 12.4 %copy-start.2 = (s32[3]{0:T(128)S(1)}, s32[3]{0:T(128)}, u32[]{:S(2)}) copy-start(s32[3]{0:T(128)} %shift_ref.1) | copy-start | bytes 40
  2.9 12.4 %copy-start.3 = (f32[128,256]{1,0:T(8,128)S(1)}, f32[128,256]{1,0:T(8,128)}, u32[]{:S(2)}) copy-start(f32[128,256]{1,0:T(8,128)} %constant.20.clone.cols_ref) | copy-start | bytes 393220
  2.9 12.4 %copy-start.8 = (s32[1,128]{1,0:T(1,128)S(1)}, s32[1,128]{1,0:T(1,128)}, u32[]{:S(2)}) copy-start(s32[1,128]{1,0:T(1,128)} %constant.31.col_ref) | copy-start | bytes 1540
  2.9 34.9 %all-to-all-start = ((f32[128,25,1,128]{3,2,1,0:T(1,128)}), f32[128,25,1,128]{3,2,1,0:T(1,128)S(1)}, u32[]{:S(2)}, u32[]{:S(2)}) async-start(f32[128,25,1,128]{3,2,1,0:T(1,128)} %bitcast.21), calls=%async_computation | async-start | bytes 3276800 | tf_op jit(solution)/shard_map/all_to_all | solution.py:258
  15.3 0.9 %copy-start.4 = (f32[256,16]{1,0:T(8,128)S(1)}, f32[256,16]{1,0:T(8,128)}, u32[]{:S(2)}) copy-start(f32[256,16]{1,0:T(8,128)} %constant.21.clone.rows_ref) | copy-start | bytes 49156
  16.2 0.8 %copy-start.5 = (f32[128,128]{1,0:T(8,128)S(1)}, f32[128,128]{1,0:T(8,128)}, u32[]{:S(2)}) copy-start(f32[128,128]{1,0:T(8,128)} %constant.22.clone.pick_ref) | copy-start | bytes 196612
  17.1 0.8 %copy-start.6 = (f32[128,128]{1,0:T(8,128)S(1)}, f32[128,128]{1,0:T(8,128)}, u32[]{:S(2)}) copy-start(f32[128,128]{1,0:T(8,128)} %constant.23.clone.picked_ref) | copy-start | bytes 196612
  17.9 0.8 %copy-start.7 = (s32[128,1]{1,0:T(8,128)S(1)}, s32[128,1]{1,0:T(8,128)}, u32[]{:S(2)}) copy-start(s32[128,1]{1,0:T(8,128)} %constant.30.row_ref) | copy-start | bytes 1540

commit v6 on v5

--- a/solution.py
+++ b/solution.py
@@ -64,7 +64,7 @@
             step = ROWS * (spots[1] - spots[0])
             message_ref[pl.ds(row, 4, stride=step), :] = joined[first : first + 4, :]
     waited, filled, sent = set(), [0] * 8, []
-    for group in (0, 2, 4, 6, 1, 3, 5, 7):
+    for group in range(8):
         if group // 4 not in waited:
             copies[group // 4].wait()
             waited.add(group // 4)
@@ -361,11 +361,11 @@
     return out.reshape(green_blocks.shape)
 
 
-def places(mesh, z_first):
+def places(mesh, y_first):
     def key(place):
         energy, momentum = divmod(place, 8)
         x, y, z = momentum % 4, energy // 4, 2 * (momentum // 4) + (energy // 2) % 2
-        return (energy % 2,) + ((z, x, y) if z_first else (x, y, z))
+        return (energy % 2,) + ((y, z, x) if y_first else (x, y, z))
 
     return sorted(range(mesh.size), key=key)
 

time: 73.1 us -> 72.9 us (level)
  waiting for transfers between devices: 14.4 us -> 15.8 us
  blocking collectives: 29.7 us -> 28.3 us
    all_to_all x1, blocking collectives: 29.7 us -> 28.3 us  [exchange(): lax.all_to_all(message.reshape(POINTS, ROWS, 1, LANES), AXES, split_axis=...]
    all_to_all x1, waiting for transfers between devices: 14.4 us -> 15.8 us  [exchange(): lax.all_to_all(message.reshape(POINTS, ROWS, 1, LANES), AXES, split_axis=...]
where the time goes in v6:
time: 72.9 us; the launch traced here: 72.5 us
  blocking collectives  28.3 us (39%)
  waiting for transfers between devices  15.8 us (22%)
  Pallas kernels  12.5 us (17%)
  starting transfers between devices  11.5 us (16%)
  local copies, waits for them, and re-layouts  3.84 us (5%)
    all_to_all x1, blocking collectives, exchange(): lax.all_to_all(message.reshape(POINTS, ROWS, 1, LANES), AXES, split_axis=...  28.3 us
    all_to_all x1, waiting for transfers between devices, exchange(): lax.all_to_all(message.reshape(POINTS, ROWS, 1, LANES), AXES, split_axis=...  15.8 us
    all_to_all x1, starting transfers between devices, exchange(): lax.all_to_all(message.reshape(POINTS, ROWS, 1, LANES), AXES, split_axis=...  11.5 us
    pallas_call x1, Pallas kernels, on_device(): pl.pallas_call(prepare_kernel, in_specs=[smem, smem] + [vmem] * 8, out_sp...  4.64 us
    unnamed x23, local copies, waits for them, and re-layouts  3.72 us
    pallas_call x1, Pallas kernels, on_device(): pl.pallas_call(compute_kernel, in_specs=[vmem] * 4, out_specs=vmem, out_s...  3.67 us
    pallas_call x1, Pallas kernels, on_device(): pl.pallas_call(functools.partial(pack_kernel, out_spots), in_specs=[hbm],...  2.6 us
    pallas_call x1, Pallas kernels, on_device(): pl.pallas_call(functools.partial(unpack_kernel, back_spots), in_specs=[vm...  1.55 us
  transfers between devices with their start and end apart: 1, of which 1 were waited for; matrix products, arithmetic and copies ran while one was open for 1% of the time, Pallas kernels for 6%

profile of v6, /device:TPU:1, one launch (start us, length us, event | category | flops | bytes accessed | tf_op | source)
XLA Modules:
  0.0 72.5 jit_solution(4193047179607042338)
XLA Ops:
  0.0 0.0 copy-start
  0.0 2.6 %pack.1 = f32[3200,128]{1,0:T(8,128)} custom-call(f32[400,1024]{1,0:T(8,128)} %bitcast.22), custom_call_target="tpu_custom_call" | custom-call | tf_op jit(solution)/shard_map/pack/pallas_call | solution.py:286
  2.6 0.0 copy-start.9
  2.6 0.0 copy-start.10
  2.6 0.0 copy-start.1
  2.6 0.0 copy-start.2
  2.7 0.0 copy-start.3
  2.7 0.0 copy-start.8
  2.7 11.5 %all-to-all-start = ((f32[128,25,1,128]{3,2,1,0:T(1,128)}), f32[128,25,1,128]{3,2,1,0:T(1,128)S(1)}, u32[]{:S(2)}, u32[]{:S(2)}) async-start(f32[128,25,1,128]{3,2,1,0:T(1,128)} %bitcast.21), calls=%async_computation | async-start | bytes 3276800 | tf_op jit(solution)/shard_map/all_to_all | solution.py:258
  14.2 0.1 reshape.28
  14.3 0.3 copy.24
  14.6 0.0 copy-done
  14.6 0.0 copy-done.10
  14.6 0.4 fusion
  15.1 0.0 copy-start.4
  15.1 0.9 %copy-done.4 = f32[256,16]{1,0:T(8,128)S(1)} copy-done((f32[256,16]{1,0:T(8,128)S(1)}, f32[256,16]{1,0:T(8,128)}, u32[]{:S(2)}) %copy-start.4) | copy-done | bytes 16408
  16.0 0.8 %copy-done.5 = f32[128,128]{1,0:T(8,128)S(1)} copy-done((f32[128,128]{1,0:T(8,128)S(1)}, f32[128,128]{1,0:T(8,128)}, u32[]{:S(2)}) %copy-start.5) | copy-done | bytes 65560
  16.8 0.8 %copy-done.6 = f32[128,128]{1,0:T(8,128)S(1)} copy-done((f32[128,128]{1,0:T(8,128)S(1)}, f32[128,128]{1,0:T(8,128)}, u32[]{:S(2)}) %copy-start.6) | copy-done | bytes 65560
  17.7 0.8 %copy-done.7 = s32[128,1]{1,0:T(8,128)S(1)} copy-done((s32[128,1]{1,0:T(8,128)S(1)}, s32[128,1]{1,0:T(8,128)}, u32[]{:S(2)}) %copy-start.7) | copy-done | bytes 536
  18.5 4.6 %prepare.1 = (bf16[24,112,256]{2,1,0:T(8,128)(2,1)S(1)}, bf16[2,384,128]{2,1,0:T(8,128)(2,1)S(1)}, bf16[2,384,128]{2,1,0:T(8,128)(2,1)S(1)}) custom-call(f32[3]{0:T(128)S(1)} %copy-done.1, s32[3]{0:T(128)S(1)} %copy-done.2, f32[384,128]{1,0:T(8,128)S(1)} %bitcast.20, f32[3,8,128]{2,1,0:T(8,128)S(1)} %pad.9.mix_ref, f32[128,256]{1,0:T(8,128)S(1)} %copy-done.3, ...), custom_call_target="tpu_custom_call" | custom-call | flops 1000000000 | bytes 4000000 | tf_op jit(solution)/shard_map/prepare/pallas_call | solution.py:314
  23.2 15.8 %all-to-all-done = f32[128,25,1,128]{3,2,1,0:T(1,128)S(1)} async-done(((f32[128,25,1,128]{3,2,1,0:T(1,128)}), f32[128,25,1,128]{3,2,1,0:T(1,128)S(1)}, u32[]{:S(2)}, u32[]{:S(2)}) %all-to-all-start) | async-done | bytes 1638432 | tf_op jit(solution)/shard_map/all_to_all | solution.py:258
  39.0 3.7 %compute.1 = f32[3200,128]{1,0:T(8,128)S(1)} custom-call(f32[3200,128]{1,0:T(8,128)S(1)} %bitcast.17, bf16[24,112,256]{2,1,0:T(8,128)(2,1)S(1)} %get-tuple-element.8.weight_ref, bf16[2,384,128]{2,1,0:T(8,128)(2,1)S(1)} %get-tuple-element.9.high_ref, bf16[2,384,128]{2,1,0:T(8,128)(2,1)S(1)} %get-tuple-element.10.low_ref), custom_call_target="tpu_custom_call" | custom-call | tf_op jit(solution)/shard_map/compute/pallas_call | solution.py:339
  42.6 28.3 %all_to_all.10 = f32[128,25,1,128]{3,2,1,0:T(1,128)S(1)} all-to-all(f32[128,25,1,128]{3,2,1,0:T(1,128)S(1)} %bitcast.18), channel_id=1, replica_groups={{0,16,4,20,32,48,36,52,64,80,68,84,96,112,100,116,1,17,5,21,33,49,37,53..., dimensions={0} | all-to-all | bytes 3276800 | tf_op jit(solution)/shard_map/all_to_all | solution.py:258
  70.9 1.6 %unpack.1 = f32[400,1024]{1,0:T(8,128)} custom-call(f32[3200,128]{1,0:T(8,128)S(1)} %bitcast.19), custom_call_target="tpu_custom_call" | custom-call | tf_op jit(solution)/shard_map/unpack/pallas_call | solution.py:348
  (11 shorter events, 0.0 us)
Async XLA Ops:
  0.0 14.6 %copy-start = (f32[8,3]{0,1:T(4,128)S(1)}, f32[8,3]{0,1:T(4,128)}, u32[]{:S(2)}) copy-start(f32[8,3]{0,1:T(4,128)} %param.16) | copy-start | bytes 292
  2.6 11.6 %copy-start.9 = (f32[3,100,8]{1,2,0:T(8,128)S(1)}, f32[3,100,8]{1,2,0:T(8,128)}, u32[]{:S(2)}) copy-start(f32[3,100,8]{1,2,0:T(8,128)} %param.13) | copy-start | bytes 28804
  2.6 12.0 %copy-start.10 = (s32[8,8]{1,0:T(8,128)S(1)}, s32[8,8]{1,0:T(8,128)}, u32[]{:S(2)}) copy-start(s32[8,8]{1,0:T(8,128)} %param.17) | copy-start | bytes 772
  2.6 12.4 %copy-start.1 = (f32[3]{0:T(128)S(1)}, f32[3]{0:T(128)}, u32[]{:S(2)}) copy-start(f32[3]{0:T(128)} %occ_ref.1) | copy-start | bytes 40
  2.6 12.4 %copy-start.2 = (s32[3]{0:T(128)S(1)}, s32[3]{0:T(128)}, u32[]{:S(2)}) copy-start(s32[3]{0:T(128)} %shift_ref.1) | copy-start | bytes 40
  2.7 12.4 %copy-start.3 = (f32[128,256]{1,0:T(8,128)S(1)}, f32[128,256]{1,0:T(8,128)}, u32[]{:S(2)}) copy-start(f32[128,256]{1,0:T(8,128)} %constant.20.clone.cols_ref) | copy-start | bytes 393220
  2.7 12.4 %copy-start.8 = (s32[1,128]{1,0:T(1,128)S(1)}, s32[1,128]{1,0:T(1,128)}, u32[]{:S(2)}) copy-start(s32[1,128]{1,0:T(1,128)} %constant.31.col_ref) | copy-start | bytes 1540
  2.7 36.3 %all-to-all-start = ((f32[128,25,1,128]{3,2,1,0:T(1,128)}), f32[128,25,1,128]{3,2,1,0:T(1,128)S(1)}, u32[]{:S(2)}, u32[]{:S(2)}) async-start(f32[128,25,1,128]{3,2,1,0:T(1,128)} %bitcast.21), calls=%async_computation | async-start | bytes 3276800 | tf_op jit(solution)/shard_map/all_to_all | solution.py:258
  15.1 0.9 %copy-start.4 = (f32[256,16]{1,0:T(8,128)S(1)}, f32[256,16]{1,0:T(8,128)}, u32[]{:S(2)}) copy-start(f32[256,16]{1,0:T(8,128)} %constant.21.clone.rows_ref) | copy-start | bytes 49156
  16.0 0.8 %copy-start.5 = (f32[128,128]{1,0:T(8,128)S(1)}, f32[128,128]{1,0:T(8,128)}, u32[]{:S(2)}) copy-start(f32[128,128]{1,0:T(8,128)} %constant.22.clone.pick_ref) | copy-start | bytes 196612
  16.8 0.8 %copy-start.6 = (f32[128,128]{1,0:T(8,128)S(1)}, f32[128,128]{1,0:T(8,128)}, u32[]{:S(2)}) copy-start(f32[128,128]{1,0:T(8,128)} %constant.23.clone.picked_ref) | copy-start | bytes 196612
  17.7 0.8 %copy-start.7 = (s32[128,1]{1,0:T(8,128)S(1)}, s32[128,1]{1,0:T(8,128)}, u32[]{:S(2)}) copy-start(s32[128,1]{1,0:T(8,128)} %constant.30.row_ref) | copy-start | bytes 1540

commit v7 on v6

--- a/solution.py
+++ b/solution.py
@@ -91,31 +91,7 @@
 
 
 def unpack_kernel(spots, in_ref, out_ref, held_ref, rest_ref, sems):
-    lane = lax.broadcasted_iota(jnp.int32, (16, LANES), 1)
-    pieces = []
-    for group in range(8):
-        rows = [ROWS * spots[16 * group + first] + 24 for first in range(0, 16, 4)]
-        step = ROWS * (spots[1] - spots[0])
-        pieces.append(
-            jnp.concatenate([in_ref[pl.ds(row, 4, stride=step), :] for row in rows], axis=0)
-        )
-    for atom in range(8):
-        joined = None
-        for group in range(8):
-            piece = turn(pieces[group], 16 * (group - atom))
-            joined = piece if joined is None else jnp.where(lane < 16 * group, joined, piece)
-        rest_ref[pl.ds(atom, 16, stride=8), :] = joined
-    turned = rest_ref[...].T
-    for group in range(8):
-        held_ref[384:400, LANES * group : LANES * (group + 1)] = turned[
-            16 * group : 16 * group + 16, :
-        ]
-    copies = [
-        pltpu.make_async_copy(
-            held_ref.at[pl.ds(384, 16), :], out_ref.at[pl.ds(384, 16), :], sems.at[8]
-        )
-    ]
-    copies[0].start()
+    copies = []
     for group in range(8):
         for tile in range(3):
             rows = [ROWS * spots[16 * group + owner] + 8 * tile for owner in range(16)]
@@ -127,6 +103,31 @@
             pltpu.make_async_copy(held_ref.at[place], out_ref.at[place], sems.at[group])
         )
         copies[-1].start()
+    lane = lax.broadcasted_iota(jnp.int32, (16, LANES), 1)
+    pieces = []
+    for group in range(8):
+        rows = [ROWS * spots[16 * group + first] + 24 for first in range(0, 16, 4)]
+        step = ROWS * (spots[1] - spots[0])
+        pieces.append(
+            jnp.concatenate([in_ref[pl.ds(row, 4, stride=step), :] for row in rows], axis=0)
+        )
+    for atom in range(8):
+        joined = None
+        for group in range(8):
+            piece = turn(pieces[group], 16 * (group - atom))
+            joined = piece if joined is None else jnp.where(lane < 16 * group, joined, piece)
+        rest_ref[pl.ds(atom, 16, stride=8), :] = joined
+    turned = rest_ref[...].T
+    for group in range(8):
+        held_ref[384:400, LANES * group : LANES * (group + 1)] = turned[
+            16 * group : 16 * group + 16, :
+        ]
+    copies.append(
+        pltpu.make_async_copy(
+            held_ref.at[pl.ds(384, 16), :], out_ref.at[pl.ds(384, 16), :], sems.at[8]
+        )
+    )
+    copies[-1].start()
     for copy in copies:
         copy.wait()
 

time: 72.9 us -> 72.8 us (level)
  no operation moved by 1% of the time
where the time goes in v7:
time: 72.8 us; the launch traced here: 72.4 us
  blocking collectives  28.3 us (39%)
  waiting for transfers between devices  15.8 us (22%)
  Pallas kernels  12.4 us (17%)
  starting transfers between devices  11.5 us (16%)
  local copies, waits for them, and re-layouts  3.84 us (5%)
    all_to_all x1, blocking collectives, exchange(): lax.all_to_all(message.reshape(POINTS, ROWS, 1, LANES), AXES, split_axis=...  28.3 us
    all_to_all x1, waiting for transfers between devices, exchange(): lax.all_to_all(message.reshape(POINTS, ROWS, 1, LANES), AXES, split_axis=...  15.8 us
    all_to_all x1, starting transfers between devices, exchange(): lax.all_to_all(message.reshape(POINTS, ROWS, 1, LANES), AXES, split_axis=...  11.5 us
    pallas_call x1, Pallas kernels, on_device(): pl.pallas_call(prepare_kernel, in_specs=[smem, smem] + [vmem] * 8, out_sp...  4.64 us
    unnamed x23, local copies, waits for them, and re-layouts  3.72 us
    pallas_call x1, Pallas kernels, on_device(): pl.pallas_call(compute_kernel, in_specs=[vmem] * 4, out_specs=vmem, out_s...  3.67 us
    pallas_call x1, Pallas kernels, on_device(): pl.pallas_call(functools.partial(pack_kernel, out_spots), in_specs=[hbm],...  2.6 us
    pallas_call x1, Pallas kernels, on_device(): pl.pallas_call(functools.partial(unpack_kernel, back_spots), in_specs=[vm...  1.47 us
  transfers between devices with their start and end apart: 1, of which 1 were waited for; matrix products, arithmetic and copies ran while one was open for 1% of the time, Pallas kernels for 6%

profile of v7, /device:TPU:1, one launch (start us, length us, event | category | flops | bytes accessed | tf_op | source)
XLA Modules:
  0.0 72.4 jit_solution(7619555968306618247)
XLA Ops:
  0.0 0.0 copy-start
  0.0 2.6 %pack.1 = f32[3200,128]{1,0:T(8,128)} custom-call(f32[400,1024]{1,0:T(8,128)} %bitcast.22), custom_call_target="tpu_custom_call" | custom-call | tf_op jit(solution)/shard_map/pack/pallas_call | solution.py:287
  2.6 0.0 copy-start.9
  2.6 0.0 copy-start.10
  2.6 0.0 copy-start.1
  2.6 0.0 copy-start.2
  2.7 0.0 copy-start.3
  2.7 0.0 copy-start.8
  2.7 11.5 %all-to-all-start = ((f32[128,25,1,128]{3,2,1,0:T(1,128)}), f32[128,25,1,128]{3,2,1,0:T(1,128)S(1)}, u32[]{:S(2)}, u32[]{:S(2)}) async-start(f32[128,25,1,128]{3,2,1,0:T(1,128)} %bitcast.21), calls=%async_computation | async-start | bytes 3276800 | tf_op jit(solution)/shard_map/all_to_all | solution.py:259
  14.2 0.1 reshape.28
  14.3 0.3 copy.24
  14.6 0.0 copy-done
  14.6 0.0 copy-done.10
  14.6 0.4 fusion
  15.1 0.0 copy-start.4
  15.1 0.9 %copy-done.4 = f32[256,16]{1,0:T(8,128)S(1)} copy-done((f32[256,16]{1,0:T(8,128)S(1)}, f32[256,16]{1,0:T(8,128)}, u32[]{:S(2)}) %copy-start.4) | copy-done | bytes 16408
  16.0 0.8 %copy-done.5 = f32[128,128]{1,0:T(8,128)S(1)} copy-done((f32[128,128]{1,0:T(8,128)S(1)}, f32[128,128]{1,0:T(8,128)}, u32[]{:S(2)}) %copy-start.5) | copy-done | bytes 65560
  16.8 0.8 %copy-done.6 = f32[128,128]{1,0:T(8,128)S(1)} copy-done((f32[128,128]{1,0:T(8,128)S(1)}, f32[128,128]{1,0:T(8,128)}, u32[]{:S(2)}) %copy-start.6) | copy-done | bytes 65560
  17.7 0.8 %copy-done.7 = s32[128,1]{1,0:T(8,128)S(1)} copy-done((s32[128,1]{1,0:T(8,128)S(1)}, s32[128,1]{1,0:T(8,128)}, u32[]{:S(2)}) %copy-start.7) | copy-done | bytes 536
  18.5 4.6 %prepare.1 = (bf16[24,112,256]{2,1,0:T(8,128)(2,1)S(1)}, bf16[2,384,128]{2,1,0:T(8,128)(2,1)S(1)}, bf16[2,384,128]{2,1,0:T(8,128)(2,1)S(1)}) custom-call(f32[3]{0:T(128)S(1)} %copy-done.1, s32[3]{0:T(128)S(1)} %copy-done.2, f32[384,128]{1,0:T(8,128)S(1)} %bitcast.20, f32[3,8,128]{2,1,0:T(8,128)S(1)} %pad.9.mix_ref, f32[128,256]{1,0:T(8,128)S(1)} %copy-done.3, ...), custom_call_target="tpu_custom_call" | custom-call | flops 1000000000 | bytes 4000000 | tf_op jit(solution)/shard_map/prepare/pallas_call | solution.py:315
  23.2 15.8 %all-to-all-done = f32[128,25,1,128]{3,2,1,0:T(1,128)S(1)} async-done(((f32[128,25,1,128]{3,2,1,0:T(1,128)}), f32[128,25,1,128]{3,2,1,0:T(1,128)S(1)}, u32[]{:S(2)}, u32[]{:S(2)}) %all-to-all-start) | async-done | bytes 1638432 | tf_op jit(solution)/shard_map/all_to_all | solution.py:259
  39.0 3.7 %compute.1 = f32[3200,128]{1,0:T(8,128)S(1)} custom-call(f32[3200,128]{1,0:T(8,128)S(1)} %bitcast.17, bf16[24,112,256]{2,1,0:T(8,128)(2,1)S(1)} %get-tuple-element.8.weight_ref, bf16[2,384,128]{2,1,0:T(8,128)(2,1)S(1)} %get-tuple-element.9.high_ref, bf16[2,384,128]{2,1,0:T(8,128)(2,1)S(1)} %get-tuple-element.10.low_ref), custom_call_target="tpu_custom_call" | custom-call | tf_op jit(solution)/shard_map/compute/pallas_call | solution.py:340
  42.6 28.3 %all_to_all.10 = f32[128,25,1,128]{3,2,1,0:T(1,128)S(1)} all-to-all(f32[128,25,1,128]{3,2,1,0:T(1,128)S(1)} %bitcast.18), channel_id=1, replica_groups={{0,16,4,20,32,48,36,52,64,80,68,84,96,112,100,116,1,17,5,21,33,49,37,53..., dimensions={0} | all-to-all | bytes 3276800 | tf_op jit(solution)/shard_map/all_to_all | solution.py:259
  70.9 1.5 %unpack.1 = f32[400,1024]{1,0:T(8,128)} custom-call(f32[3200,128]{1,0:T(8,128)S(1)} %bitcast.19), custom_call_target="tpu_custom_call" | custom-call | tf_op jit(solution)/shard_map/unpack/pallas_call | solution.py:349
  (11 shorter events, 0.0 us)
Async XLA Ops:
  0.0 14.6 %copy-start = (f32[8,3]{0,1:T(4,128)S(1)}, f32[8,3]{0,1:T(4,128)}, u32[]{:S(2)}) copy-start(f32[8,3]{0,1:T(4,128)} %param.16) | copy-start | bytes 292
  2.6 11.6 %copy-start.9 = (f32[3,100,8]{1,2,0:T(8,128)S(1)}, f32[3,100,8]{1,2,0:T(8,128)}, u32[]{:S(2)}) copy-start(f32[3,100,8]{1,2,0:T(8,128)} %param.13) | copy-start | bytes 28804
  2.6 12.0 %copy-start.10 = (s32[8,8]{1,0:T(8,128)S(1)}, s32[8,8]{1,0:T(8,128)}, u32[]{:S(2)}) copy-start(s32[8,8]{1,0:T(8,128)} %param.17) | copy-start | bytes 772
  2.6 12.4 %copy-start.1 = (f32[3]{0:T(128)S(1)}, f32[3]{0:T(128)}, u32[]{:S(2)}) copy-start(f32[3]{0:T(128)} %occ_ref.1) | copy-start | bytes 40
  2.6 12.4 %copy-start.2 = (s32[3]{0:T(128)S(1)}, s32[3]{0:T(128)}, u32[]{:S(2)}) copy-start(s32[3]{0:T(128)} %shift_ref.1) | copy-start | bytes 40
  2.7 12.4 %copy-start.3 = (f32[128,256]{1,0:T(8,128)S(1)}, f32[128,256]{1,0:T(8,128)}, u32[]{:S(2)}) copy-start(f32[128,256]{1,0:T(8,128)} %constant.20.clone.cols_ref) | copy-start | bytes 393220
  2.7 12.4 %copy-start.8 = (s32[1,128]{1,0:T(1,128)S(1)}, s32[1,128]{1,0:T(1,128)}, u32[]{:S(2)}) copy-start(s32[1,128]{1,0:T(1,128)} %constant.31.col_ref) | copy-start | bytes 1540
  2.7 36.3 %all-to-all-start = ((f32[128,25,1,128]{3,2,1,0:T(1,128)}), f32[128,25,1,128]{3,2,1,0:T(1,128)S(1)}, u32[]{:S(2)}, u32[]{:S(2)}) async-start(f32[128,25,1,128]{3,2,1,0:T(1,128)} %bitcast.21), calls=%async_computation | async-start | bytes 3276800 | tf_op jit(solution)/shard_map/all_to_all | solution.py:259
  15.1 0.9 %copy-start.4 = (f32[256,16]{1,0:T(8,128)S(1)}, f32[256,16]{1,0:T(8,128)}, u32[]{:S(2)}) copy-start(f32[256,16]{1,0:T(8,128)} %constant.21.clone.rows_ref) | copy-start | bytes 49156
  16.0 0.8 %copy-start.5 = (f32[128,128]{1,0:T(8,128)S(1)}, f32[128,128]{1,0:T(8,128)}, u32[]{:S(2)}) copy-start(f32[128,128]{1,0:T(8,128)} %constant.22.clone.pick_ref) | copy-start | bytes 196612
  16.8 0.8 %copy-start.6 = (f32[128,128]{1,0:T(8,128)S(1)}, f32[128,128]{1,0:T(8,128)}, u32[]{:S(2)}) copy-start(f32[128,128]{1,0:T(8,128)} %constant.23.clone.picked_ref) | copy-start | bytes 196612
  17.7 0.8 %copy-start.7 = (s32[128,1]{1,0:T(8,128)S(1)}, s32[128,1]{1,0:T(8,128)}, u32[]{:S(2)}) copy-start(s32[128,1]{1,0:T(8,128)} %constant.30.row_ref) | copy-start | bytes 1540
